TPU v7x, 32 devices: a whole 2x2x4 slice. The times are simulated.
32 devices in a mesh: canvas: 4 (over y, x), rows: 8 (over z, core).
Axes of the slice: x: 2, y: 2, z: 4, core: 2. Of those that a mesh axis runs over, the one named last changes fastest.
Arguments:
- inputs: bfloat16 [4, 32, 384, 64], P('canvas', 'rows'), may hold values from -6 to 6
- coarse: bfloat16 [4, 16, 192, 256], P('canvas', 'rows'), may hold values from -6 to 6
- row_cuts: int32 [4, 32], P('canvas'), may hold values 0 or 1
- col_cuts: int32 [4, 384], P('canvas'), may hold values 0 or 1
- w_first: bfloat16 [3, 3, 64, 128], replicated, may hold values from -0.25 to 0.25
- b_first: bfloat16 [128], replicated, may hold values from -3 to 3
- w_second: bfloat16 [3, 3, 128, 128], replicated, may hold values from -0.1875 to 0.1875
- b_second: bfloat16 [128], replicated, may hold values from -3 to 3
- w_up: bfloat16 [2, 2, 256, 128], replicated, may hold values from -0.375 to 0.375
- b_up: bfloat16 [128], replicated, may hold values from -3 to 3
- w_third: bfloat16 [3, 3, 256, 128], replicated, may hold values from -0.125 to 0.125
- b_third: bfloat16 [128], replicated, may hold values from -3 to 3
- w_fourth: bfloat16 [3, 3, 128, 128], replicated, may hold values from -0.1875 to 0.1875
- b_fourth: bfloat16 [128], replicated, may hold values from -3 to 3
- cot_out: bfloat16 [4, 32, 384, 128], P('canvas', 'rows'), may hold values from -6 to 6
- cot_pool: bfloat16 [4, 16, 192, 128], P('canvas', 'rows'), may hold values from -12 to 12
Outputs:
- activations: bfloat16 [4, 32, 384, 128], P('canvas', 'rows')
- pooled: bfloat16 [4, 16, 192, 128], P('canvas', 'rows')
- grad_inputs: bfloat16 [4, 32, 384, 64], P('canvas', 'rows')
- grad_coarse: bfloat16 [4, 16, 192, 256], P('canvas', 'rows')
- grad_w_first: float32 [3, 3, 64, 128], P(None, None, None, 'rows')
- grad_b_first: float32 [128], P('rows')
- grad_w_second: float32 [3, 3, 128, 128], P(None, None, None, 'rows')
- grad_b_second: float32 [128], P('rows')
- grad_w_up: float32 [2, 2, 256, 128], P(None, None, None, 'rows')
- grad_b_up: float32 [128], P('rows')
- grad_w_third: float32 [3, 3, 256, 128], P(None, None, None, 'rows')
- grad_b_third: float32 [128], P('rows')
- grad_w_fourth: float32 [3, 3, 128, 128], P(None, None, None, 'rows')
- grad_b_fourth: float32 [128], P('rows')
All inputs are finite; a program needn't handle non-finite values. No bound on the sum of `row_cuts` or of `col_cuts` on one device may be relied on, other than what follows from the above.
Results may differ from a plain program's by a relative error of at most 0.013.
Values may be sent and summed in bfloat16 or wider, within the bound.
A program may use at most 64 MiB of HBM per device.

v0:
```python
import functools

import jax
import jax.numpy as jnp
from jax import lax
from jax.experimental import pallas as pl
from jax.experimental.pallas import tpu as pltpu
from jax.sharding import PartitionSpec as P

MESH = pl.DeviceIdType.MESH
BF = jnp.bfloat16
F32 = jnp.float32
VMEM_BYTES = 58 * 2**20

OPERANDS = (
    "inputs",
    "coarse",
    "row_cuts",
    "col_cuts",
    "w_first",
    "b_first",
    "w_second",
    "b_second",
    "w_up",
    "b_up",
    "w_third",
    "b_third",
    "w_fourth",
    "b_fourth",
    "cot_out",
    "cot_pool",
)
LAYERS = ("fourth", "third", "up", "second", "first")


def dot_nn(a, b):
    return lax.dot_general(a, b, (((1,), (0,)), ((), ())), preferred_element_type=F32)


def dot_tn(a, b):
    return lax.dot_general(a, b, (((0,), (0,)), ((), ())), preferred_element_type=F32)


def dot_nt(a, b):
    return lax.dot_general(a, b, (((1,), (1,)), ((), ())), preferred_element_type=F32)


def silu_and_slope(values):
    sigma = 0.5 * jnp.tanh(0.5 * values) + 0.5
    act = values * sigma
    return act, sigma + act * (1.0 - sigma)


def level_kernel(names, sizes, *refs):
    ref = dict(zip(names, refs))
    width, ch, c_in, c_coarse, rows_n, canvas_n, fused = sizes
    half = width // 2
    c = lax.axis_index("canvas")
    r = lax.axis_index("rows")
    z, k = r // 2, lax.rem(r, 2)
    up_id, down_id = (c, r - 1), (c, r + 1)
    has_up, has_down = r > 0, r < rows_n - 1
    z_n = rows_n // 2

    barrier = pltpu.get_barrier_semaphore()

    def greet(device):
        pl.semaphore_signal(barrier, inc=1, device_id=device, device_id_type=MESH)

    pl.when(has_up)(lambda: greet(up_id))
    pl.when(has_down)(lambda: greet(down_id))
    if fused:
        for step in range(1, z_n):
            greet((c, lax.rem(z + step, z_n) * 2 + k))
        for step in range(1, canvas_n):
            greet((lax.rem(c + step, canvas_n), r))

    local_sem = ref["local_sem"]
    used = [0]

    def fetch(src, dst):
        copy = pltpu.make_async_copy(src, dst, local_sem.at[used[0]])
        used[0] += 1
        copy.start()
        return copy

    X, CO = ref["X"], ref["CO"]
    in_x = fetch(ref["inputs"].at[0], X.at[pl.ds(4, 4)])
    in_w1 = fetch(ref["w_first"], ref["KB1"].at[pl.ds(1, 3)])
    in_co = fetch(ref["coarse"].at[0], CO.at[pl.ds(1, 2)])
    in_up = [
        fetch(ref["w_up"].at[a, b], ref["WU"].at[:, pl.ds((2 * a + b) * ch, ch)])
        for a in (0, 1)
        for b in (0, 1)
    ]
    in_w2 = fetch(ref["w_second"], ref["KB2"].at[pl.ds(1, 3)])
    in_w3 = fetch(ref["w_third"], ref["KB3"].at[pl.ds(1, 3)])
    in_w4 = fetch(ref["w_fourth"], ref["KB4"].at[pl.ds(1, 3)])
    in_cot = fetch(ref["cot_out"].at[0], ref["COT"])
    in_cp = fetch(ref["cot_pool"].at[0], ref["CP"])

    first, total_rows = r * 4, rows_n * 4

    def link(h):
        row = first + h
        inside = jnp.logical_and(row > 0, row < total_rows)
        cut = ref["row_cuts"][0, jnp.clip(row, 0, total_rows - 1)]
        return jnp.where(inside, 1 - cut, 0)

    open_row = 1.0 - ref["col_cuts"][...].astype(F32)
    open_row = jnp.where(lax.broadcasted_iota(jnp.int32, (1, width), 1) > 0, open_row, 0.0)
    left_gate = jnp.broadcast_to(open_row, (128, width))
    right_gate = pltpu.roll(left_gate, width - 1, 1)
    GL, GR = ref["GL"], ref["GR"]
    GL[...] = left_gate.T
    GR[...] = right_gate.T
    left_row, right_row = left_gate[:c_in], right_gate[:c_in]

    for name in ("KB1", "KB2", "KB3", "KB4"):
        ref[name][0] = jnp.zeros(ref[name].shape[1:], BF)
    for name in ("KT1", "KT2", "KT4", "VA", "VJ", "VC"):
        ref[name][0] = jnp.zeros(ref[name].shape[1:], BF)
    ref["KT3"][0] = jnp.zeros(ref["KT3"].shape[1:], BF)
    X[12] = jnp.zeros(X.shape[1:], BF)

    halo_send, halo_recv = ref["halo_send"], ref["halo_recv"]

    def remote(src, dst, send, recv, device):
        return pltpu.make_async_remote_copy(
            src_ref=src, dst_ref=dst, send_sem=send, recv_sem=recv, device_id=device, device_id_type=MESH
        )

    def pair_exchange(index, src_up, dst_up, src_down, dst_down):
        to_up = remote(src_up, dst_up, halo_send.at[index, 0], halo_recv.at[index, 0], up_id)
        to_down = remote(src_down, dst_down, halo_send.at[index, 1], halo_recv.at[index, 1], down_id)
        return to_up, to_down

    def start_exchange(pair):
        pl.when(has_up)(lambda: pair[0].start())
        pl.when(has_down)(lambda: pair[1].start())

    def receive(pair):
        pl.when(has_down)(lambda: pair[0].wait_recv())
        pl.when(has_up)(lambda: pair[1].wait_recv())

    def sent(pair):
        pl.when(has_up)(lambda: pair[0].wait_send())
        pl.when(has_down)(lambda: pair[1].wait_send())

    G4, G2 = ref["G4"], ref["G2"]
    x_halo = pair_exchange(0, ref["inputs"].at[0], X.at[pl.ds(8, 4)], ref["inputs"].at[0], X.at[pl.ds(0, 4)])
    co_halo = pair_exchange(1, ref["coarse"].at[0, 0], CO.at[3], ref["coarse"].at[0, 1], CO.at[0])
    g4_halo = pair_exchange(2, G4.at[pl.ds(2, 2)], G4.at[pl.ds(6, 2)], G4.at[pl.ds(4, 2)], G4.at[pl.ds(0, 2)])
    g2_halo = pair_exchange(3, G2.at[pl.ds(2, 2)], G2.at[pl.ds(6, 2)], G2.at[pl.ds(4, 2)], G2.at[pl.ds(0, 2)])

    @pl.when(jnp.logical_not(has_up))
    def _():
        X[0:4] = jnp.zeros((4,) + X.shape[1:], BF)
        CO[0] = jnp.zeros(CO.shape[1:], BF)
        G4[0:2] = jnp.zeros((2,) + G4.shape[1:], BF)
        G2[0:2] = jnp.zeros((2,) + G2.shape[1:], BF)

    @pl.when(jnp.logical_not(has_down))
    def _():
        X[8:12] = jnp.zeros((4,) + X.shape[1:], BF)
        CO[3] = jnp.zeros(CO.shape[1:], BF)
        G4[6:8] = jnp.zeros((2,) + G4.shape[1:], BF)
        G2[6:8] = jnp.zeros((2,) + G2.shape[1:], BF)

    peers = (z_n - 1 + canvas_n - 1) if fused else 0
    pl.semaphore_wait(barrier, peers + has_up.astype(jnp.int32) + has_down.astype(jnp.int32))
    start_exchange(x_halo)
    start_exchange(co_halo)

    def widen(value):
        left = (pltpu.roll(value, 1, 0) * GL[...]).astype(BF)
        right = (pltpu.roll(value, width - 1, 0) * GR[...]).astype(BF)
        return left, value.astype(BF), right

    def put_wide(dst, row, value, base=0, stride=ch):
        for place, piece in enumerate(widen(value)):
            lo = base + place * stride
            dst[row, :, lo : lo + ch] = piece

    def taps(bank, h):
        ga, gb, gc = link(h), link(h + 1), link(h + 2)
        return bank[0], bank[ga], bank[2], bank[gb * 3], bank[gb], bank[gc * 3]

    def conv_pair(src, at, bank, h):
        band = jnp.concatenate([src[at + d] for d in (-1, 0, 1, 2)], axis=1)
        zero, up0, mid, down0, up1, down1 = taps(bank, h)
        weights = jnp.concatenate(
            [
                jnp.concatenate([up0, mid, down0, zero], axis=0),
                jnp.concatenate([zero, up1, mid, down1], axis=0),
            ],
            axis=1,
        )
        return dot_nn(band, weights)

    def back_weights(bank, h):
        zero, up0, mid, down0, up1, down1 = taps(bank, h)
        return jnp.concatenate(
            [
                jnp.concatenate([up0, mid, down0, zero], axis=1),
                jnp.concatenate([zero, up1, mid, down1], axis=1),
            ],
            axis=0,
        )

    def back_pair(src, at, bank, h):
        band = jnp.concatenate([src[at + d] for d in (-1, 0, 1, 2)], axis=1)
        return dot_nt(band, back_weights(bank, h))

    def bias(name):
        return ref[name][...].astype(F32).reshape(1, ch)

    V3X, V3A, V3J, V3C = ref["V3X"], ref["V3A"], ref["V3J"], ref["V3C"]
    VA, VJ, VC = ref["VA"], ref["VJ"], ref["VC"]
    S1, S2, S3 = ref["S1"], ref["S2"], ref["S3"]
    KB1, KB2, KB3, KB4 = ref["KB1"], ref["KB2"], ref["KB3"], ref["KB4"]
    KT1, KT2, KT3, KT4 = ref["KT1"], ref["KT2"], ref["KT3"], ref["KT4"]

    def widen_input(row):
        value = X[row].astype(F32)
        V3X[row, 0:c_in] = (pltpu.roll(value, 1, 1) * left_row).astype(BF)
        V3X[row, c_in : 2 * c_in] = X[row]
        V3X[row, 2 * c_in : 3 * c_in] = (pltpu.roll(value, width - 1, 1) * right_row).astype(BF)

    b_first, b_second, b_up, b_third, b_fourth = (
        bias("b_" + name) for name in ("first", "second", "up", "third", "fourth")
    )

    def first_pair(h):
        at = h + 4
        band = V3X[pl.ds(at - 1, 4)].reshape(4 * 3 * c_in, width)
        zero, up0, mid, down0, up1, down1 = [t.reshape(3 * c_in, ch) for t in taps(KB1, h)]
        weights = jnp.concatenate(
            [
                jnp.concatenate([up0, mid, down0, zero], axis=0),
                jnp.concatenate([zero, up1, mid, down1], axis=0),
            ],
            axis=1,
        )
        both = dot_tn(band, weights)
        for j in (0, 1):
            act, slope = silu_and_slope(both[:, j * ch : (j + 1) * ch] + b_first)
            S1[h + j + 3] = slope
            put_wide(V3A, h + j + 3, act)
            VA[h + j + 4] = act.astype(BF)

    in_x.wait()
    in_w1.wait()
    for row in (4, 5, 6, 7):
        widen_input(row)
    first_pair(1)

    SA, SB = ref["SA"], ref["SB"]
    WU = ref["WU"]

    def up_rows(i):
        fine = dot_nn(CO[i], WU[...])
        for a in (0, 1):
            for b in (0, 1):
                lo = (2 * a + b) * ch
                piece = (fine[:, lo : lo + ch] + b_up).astype(BF).astype(F32)
                SA[a, pl.ds(b, half, stride=2), :] = piece
        for a in (0, 1):
            value = SA[a]
            put_wide(V3J, 2 * i + a, value, base=0, stride=2 * ch)
            VJ[2 * i + a + 1, :, :ch] = value.astype(BF)

    in_co.wait()
    for copy in in_up:
        copy.wait()
    up_rows(1)
    up_rows(2)

    in_w2.wait()
    in_w3.wait()
    in_w4.wait()
    for bank, back, part in ((KB1, KT1, c_in), (KB2, KT2, ch), (KB3, KT3, 2 * ch), (KB4, KT4, ch)):
        for row_tap in range(3):
            for col_tap in range(3):
                back[1 + (2 - row_tap), :, (2 - col_tap) * ch : (3 - col_tap) * ch] = bank[
                    1 + row_tap, col_tap * part : (col_tap + 1) * part
                ]

    receive(x_halo)
    for row in (0, 1, 2, 3, 8, 9, 10, 11):
        widen_input(row)
    for h in (-1, 3, -3, 5):
        first_pair(h)

    pooled_buf = ref["POOL"]

    def second_pair(h):
        both = conv_pair(V3A, h + 3, KB2, h)
        acts = []
        for j in (0, 1):
            act, slope = silu_and_slope(both[:, j * ch : (j + 1) * ch] + b_second)
            if 0 <= h + j < 4:
                S2[h + j] = slope
            put_wide(V3J, h + j + 2, act, base=ch, stride=2 * ch)
            rounded = act.astype(BF)
            VJ[h + j + 3, :, ch:] = rounded
            acts.append(rounded.astype(F32))
        if 0 <= h < 4:
            SB[...] = acts[0] + acts[1]
            pooled_buf[h // 2] = (
                (SB[pl.ds(0, half, stride=2), :] + SB[pl.ds(1, half, stride=2), :]) * 0.25
            ).astype(BF)

    for h in (0, 2, -2, 4):
        second_pair(h)
    out_pool = fetch(pooled_buf, ref["pooled"].at[0])

    receive(co_halo)
    up_rows(0)
    up_rows(3)

    def third_pair(h):
        both = conv_pair(V3J, h + 2, KB3, h)
        for j in (0, 1):
            act, slope = silu_and_slope(both[:, j * ch : (j + 1) * ch] + b_third)
            S3[h + j + 1] = slope
            put_wide(V3C, h + j + 1, act)
            VC[h + j + 2] = act.astype(BF)

    for h in (1, -1, 3):
        third_pair(h)

    G34, G33, G32, G31 = ref["G34"], ref["G33"], ref["G32"], ref["G31"]
    DB = ref["DB"]
    COT, ACT = ref["COT"], ref["ACT"]
    in_cot.wait()
    in_cp.wait()
    sums = {}

    def add_sum(name, value):
        part = jnp.sum(value.reshape(-1, 8, ch), axis=0)
        sums[name] = part if name not in sums else sums[name] + part

    def fourth_pair(h):
        both = conv_pair(V3C, h + 1, KB4, h)
        for j in (0, 1):
            act, slope = silu_and_slope(both[:, j * ch : (j + 1) * ch] + b_fourth)
            ACT[h + j] = act.astype(BF)
            g = (COT[h + j].astype(F32) * slope).astype(BF)
            G4[h + j + 2] = g
            g = g.astype(F32)
            add_sum("fourth", g)
            put_wide(G34, h + j + 2, g)

    fourth_pair(0)
    pl.when(has_up)(lambda: g4_halo[0].start())
    fourth_pair(2)
    pl.when(has_down)(lambda: g4_halo[1].start())
    out_act = fetch(ACT, ref["activations"].at[0])

    partner = (c, r + 1 - 2 * k)

    class Reduction:
        def __init__(self, index, name):
            self.index, self.name = index, name
            self.part, self.twin = ref["P_" + name], ref["RA_" + name]
            self.sums, self.along = ref["Q_" + name], ref["RB_" + name]
            self.slots = ref["RC_" + name]
            self.send, self.recv = ref["red_send"], ref["red_recv"]

        def copies_z(self):
            found = []
            for step in range(1, z_n):
                other = lax.rem(z + step, z_n)
                source = lax.rem(z + z_n - step, z_n)
                found.append(
                    remote(
                        self.sums.at[other], self.along.at[z], self.send.at[self.index, step],
                        self.recv.at[self.index, step], (c, other * 2 + k),
                    )
                )
            return found

        def copies_canvas(self):
            found = []
            for step in range(1, canvas_n):
                other = lax.rem(c + step, canvas_n)
                found.append(
                    remote(
                        self.along.at[z], self.slots.at[c], self.send.at[self.index, z_n + step],
                        self.recv.at[self.index, z_n + step], (other, r),
                    )
                )
            return found

        def start_core(self):
            if not fused:
                return
            self.core = remote(
                self.part.at[1 - k], self.twin, self.send.at[self.index, 0], self.recv.at[self.index, 0], partner
            )
            self.core.start()

        def start_z(self):
            if not fused:
                return
            self.core.wait_recv()
            self.sums[...] = (self.part[k].astype(F32) + self.twin[...].astype(F32)).astype(self.sums.dtype)
            self.along_copies = self.copies_z()
            for copy in self.along_copies:
                copy.start()

        def start_canvas(self):
            if not fused:
                return
            for copy in self.along_copies:
                copy.wait()
            self.along[z] = self.sums[z]
            total = self.along[0].astype(F32)
            for place in range(1, z_n):
                total = total + self.along[place].astype(F32)
            self.along[z] = total.astype(self.along.dtype)
            self.canvas = self.copies_canvas()
            for copy in self.canvas:
                copy.start()
            self.own = fetch(self.along.at[z], self.slots.at[c])

        def finish(self):
            if not fused:
                fetch(self.part, self.slots).wait()
                return
            self.core.wait_send()
            for copy in self.canvas:
                copy.wait()
            self.own.wait()

    red = {name: Reduction(index, name) for index, name in enumerate(LAYERS + ("bias",))}

    def put_parts(name, value):
        part = ref["P_" + name]
        blocks, share = part.shape[2], part.shape[3]
        for block in range(blocks):
            place = block if name == "up" else blocks - 1 - block
            for owner in range(8):
                lo = block * ch + owner * share
                part[owner % 2, owner // 2, place] = value[lo : lo + share].astype(BF)

    def row_stack(src, off, h):
        return jnp.concatenate(
            [src[link(h) * (h - 1 + off)], src[h + off], src[link(h + 1) * (h + 1 + off)]], axis=1
        )

    def weight_grad(grad3, at, src, off):
        band = grad3[pl.ds(at, 4)].reshape(4 * width, 3 * ch)
        stacked = jnp.concatenate([row_stack(src, off, h) for h in range(4)], axis=0)
        return dot_tn(band, stacked)

    def load_wide(dst, row, src):
        put_wide(dst, row, src.astype(F32))

    def third_back(h):
        both = back_pair(G34, h + 2, KT4, h)
        for j in (0, 1):
            g = (both[:, j * ch : (j + 1) * ch] * S3[h + j + 1]).astype(BF).astype(F32)
            if 0 <= h + j < 4:
                add_sum("third", g)
            put_wide(G33, h + j + 1, g)

    put_parts("fourth", weight_grad(G34, 2, VC, 2))
    red["fourth"].start_core()
    third_back(1)
    receive(g4_halo)
    for row in (0, 1, 6, 7):
        load_wide(G34, row, G4[row])
    third_back(-1)
    third_back(3)
    red["fourth"].start_z()

    GB, CP = ref["GB"], ref["CP"]

    def joined_back(h):
        band = jnp.concatenate([G33[h + 1 + d] for d in (-1, 0, 1)], axis=1)
        weights = jnp.concatenate([KT3[link(h)], KT3[2], KT3[link(h + 1) * 3]], axis=1)
        d_joined = dot_nt(band, weights)
        g_up = d_joined[:, :ch].astype(BF).astype(F32)
        add_sum("up", g_up)
        a = h % 2
        SA[a] = g_up
        for b in (0, 1):
            lo = (2 * a + b) * ch
            GB[h // 2, :, lo : lo + ch] = SA[a, pl.ds(b, half, stride=2), :].astype(BF)
        if a == 0:
            spread = CP[h // 2].astype(F32) * 0.25
            SB[pl.ds(0, half, stride=2), :] = spread
            SB[pl.ds(1, half, stride=2), :] = spread
        g = ((d_joined[:, ch:] + SB[...]) * S2[h]).astype(BF)
        G2[h + 2] = g
        g = g.astype(F32)
        add_sum("second", g)
        put_wide(G32, h + 2, g)

    joined_back(0)
    joined_back(1)
    pl.when(has_up)(lambda: g2_halo[0].start())
    joined_back(2)
    joined_back(3)
    pl.when(has_down)(lambda: g2_halo[1].start())

    put_parts("third", weight_grad(G33, 1, VJ, 3))
    red["third"].start_core()
    red["fourth"].start_canvas()
    bands = GB[...].reshape(2 * half, 4 * ch)
    put_parts("up", dot_tn(bands, CO[1:3].reshape(2 * half, c_coarse)))
    red["up"].start_core()
    red["third"].start_z()
    put_parts("second", weight_grad(G32, 2, VA, 4))
    red["second"].start_core()
    red["up"].start_z()

    def first_back(h):
        both = back_pair(G32, h + 2, KT2, h)
        for j in (0, 1):
            g = (both[:, j * ch : (j + 1) * ch] * S1[h + j + 3]).astype(BF).astype(F32)
            if 0 <= h + j < 4:
                add_sum("first", g)
            put_wide(G31, h + j + 1, g)

    first_back(1)
    receive(g2_halo)
    for row in (0, 1, 6, 7):
        load_wide(G32, row, G2[row])
    first_back(-1)
    first_back(3)

    def pick(h, joined):
        return X[12 + joined * (h - 8)]

    stacked = jnp.concatenate(
        [
            jnp.concatenate([pick(h - 1, link(h)), X[h + 4], pick(h + 1, link(h + 1))], axis=0)
            for h in range(4)
        ],
        axis=1,
    )
    put_parts("first", dot_nn(stacked, G31[1:5].reshape(4 * width, 3 * ch)).T)
    red["first"].start_core()
    for place, name in enumerate(("first", "second", "up", "third", "fourth")):
        DB[place : place + 1] = jnp.sum(sums[name], axis=0, keepdims=True)
    if fused:
        ref["P_bias"][0] = DB[...]
        ref["P_bias"][1] = DB[...]
    else:
        ref["P_bias"][0] = DB[...]
    red["bias"].start_core()
    red["second"].start_z()

    GI = ref["GI"]

    def input_back(h):
        weights = back_weights(KT1, h)
        band = jnp.concatenate([G31[h + 1 + d] for d in (-1, 0, 1, 2)], axis=1)
        both = dot_nt(weights, band).astype(BF)
        GI[h] = both[:c_in]
        GI[h + 1] = both[c_in:]

    red["first"].start_z()
    input_back(0)
    input_back(2)
    out_gi = fetch(GI, ref["grad_inputs"].at[0])
    GC = ref["GC"]
    for i in (0, 1):
        GC[i] = dot_nt(GB[i], WU[...]).astype(BF)
    out_gc = fetch(GC, ref["grad_coarse"].at[0])
    red["third"].start_canvas()
    red["up"].start_canvas()
    red["second"].start_canvas()

    if fused:
        bias_red = red["bias"]
        bias_red.core.wait_recv()
        bias_red.sums[z] = bias_red.part[k] + bias_red.twin[...]
        bias_red.along_copies = []
        for step in range(1, z_n):
            other = lax.rem(z + step, z_n)
            bias_red.along_copies.append(
                remote(
                    bias_red.sums.at[z], bias_red.along.at[z], bias_red.send.at[bias_red.index, step],
                    bias_red.recv.at[bias_red.index, step], (c, other * 2 + k),
                )
            )
        for copy in bias_red.along_copies:
            copy.start()
    red["first"].start_canvas()
    red["bias"].start_canvas()

    for name in LAYERS + ("bias",):
        red[name].finish()
    for pair in (x_halo, co_halo, g4_halo, g2_halo):
        sent(pair)
    for copy in (out_pool, out_act, out_gi, out_gc):
        copy.wait()


def finish_kernel(names, sizes, *refs):
    ref = dict(zip(names, refs))
    ch, share = sizes
    r = lax.axis_index("rows")
    copies = []
    for place, name in enumerate(("activations", "pooled", "grad_inputs", "grad_coarse")):
        copy = pltpu.make_async_copy(ref[name], ref["out_" + name], ref["sem"].at[place])
        copy.start()
        copies.append(copy)

    def total(slots):
        value = slots[0].astype(F32)
        for place in range(1, slots.shape[0]):
            value = value + slots[place].astype(F32)
        return value

    for name in ("first", "second", "third", "fourth"):
        value = total(ref["RC_" + name])
        out = ref["out_w_" + name]
        part = out.shape[3]
        for row_tap in range(3):
            out[row_tap] = value[:, :, row_tap * part : (row_tap + 1) * part]
    value = total(ref["RC_up"])
    for a in (0, 1):
        for b in (0, 1):
            ref["out_w_up"][a, b] = value[2 * a + b]
    sums = pltpu.roll(total(ref["RC_bias"]), lax.rem(ch - r * share, ch), 1)
    for place, name in enumerate(("first", "second", "up", "third", "fourth")):
        ref["out_b_" + name][...] = sums[place : place + 1, :share]
    for copy in copies:
        copy.wait()


def on_device(fused, rows_n, canvas_n, *args):
    arg = dict(zip(OPERANDS, args))
    _, length, width, c_in = arg["inputs"].shape
    ch = arg["w_first"].shape[3]
    c_coarse = arg["coarse"].shape[3]
    half = width // 2
    assert length == 4
    arg["inputs"] = jnp.swapaxes(arg["inputs"], 2, 3)
    arg["w_first"] = arg["w_first"].reshape(3, 3 * c_in, ch)
    arg["w_second"] = arg["w_second"].reshape(3, 3 * ch, ch)
    arg["w_third"] = arg["w_third"].reshape(3, 6 * ch, ch)
    arg["w_fourth"] = arg["w_fourth"].reshape(3, 3 * ch, ch)
    for name in ("b_first", "b_second", "b_up", "b_third", "b_fourth"):
        arg[name] = arg[name].reshape(1, ch)

    any_spec = pl.BlockSpec(memory_space=pl.ANY)
    vmem_spec = pl.BlockSpec(memory_space=pltpu.VMEM)
    in_specs = []
    for name in OPERANDS:
        if name == "row_cuts":
            in_specs.append(pl.BlockSpec(memory_space=pltpu.SMEM))
        elif name == "col_cuts" or name.startswith("b_"):
            in_specs.append(vmem_spec)
        else:
            in_specs.append(any_spec)

    owners, z_n = 8, 4
    share = ch // owners
    pieces = {
        "fourth": ((3, share, 3 * ch), BF),
        "third": ((3, share, 6 * ch), BF),
        "up": ((4, share, c_coarse), BF),
        "second": ((3, share, 3 * ch), BF),
        "first": ((3, share, 3 * c_in), BF),
        "bias": ((8, ch), F32),
    }
    outs = {
        "activations": jax.ShapeDtypeStruct((1, 4, width, ch), BF),
        "pooled": jax.ShapeDtypeStruct((1, 2, half, ch), BF),
        "grad_inputs": jax.ShapeDtypeStruct((1, 4, c_in, width), BF),
        "grad_coarse": jax.ShapeDtypeStruct((1, 2, half, c_coarse), BF),
    }
    scratch = {
        "X": pltpu.VMEM((13, c_in, width), BF),
        "CO": pltpu.VMEM((4, half, c_coarse), BF),
        "COT": pltpu.VMEM((4, width, ch), BF),
        "CP": pltpu.VMEM((2, half, ch), BF),
        "WU": pltpu.VMEM((c_coarse, 4 * ch), BF),
        "GL": pltpu.VMEM((width, ch), F32),
        "GR": pltpu.VMEM((width, ch), F32),
        "KB1": pltpu.VMEM((4, 3 * c_in, ch), BF),
        "KB2": pltpu.VMEM((4, 3 * ch, ch), BF),
        "KB3": pltpu.VMEM((4, 6 * ch, ch), BF),
        "KB4": pltpu.VMEM((4, 3 * ch, ch), BF),
        "KT1": pltpu.VMEM((4, c_in, 3 * ch), BF),
        "KT2": pltpu.VMEM((4, ch, 3 * ch), BF),
        "KT3": pltpu.VMEM((4, 2 * ch, 3 * ch), BF),
        "KT4": pltpu.VMEM((4, ch, 3 * ch), BF),
        "V3X": pltpu.VMEM((12, 3 * c_in, width), BF),
        "V3A": pltpu.VMEM((10, width, 3 * ch), BF),
        "V3J": pltpu.VMEM((8, width, 6 * ch), BF),
        "V3C": pltpu.VMEM((6, width, 3 * ch), BF),
        "VA": pltpu.VMEM((11, width, ch), BF),
        "VJ": pltpu.VMEM((9, width, 2 * ch), BF),
        "VC": pltpu.VMEM((7, width, ch), BF),
        "S1": pltpu.VMEM((10, width, ch), F32),
        "S2": pltpu.VMEM((4, width, ch), F32),
        "S3": pltpu.VMEM((6, width, ch), F32),
        "G4": pltpu.VMEM((8, width, ch), BF),
        "G2": pltpu.VMEM((8, width, ch), BF),
        "G34": pltpu.VMEM((8, width, 3 * ch), BF),
        "G33": pltpu.VMEM((6, width, 3 * ch), BF),
        "G32": pltpu.VMEM((8, width, 3 * ch), BF),
        "G31": pltpu.VMEM((6, width, 3 * ch), BF),
        "GB": pltpu.VMEM((2, half, 4 * ch), BF),
        "SA": pltpu.VMEM((2, width, ch), F32),
        "SB": pltpu.VMEM((width, ch), F32),
        "DB": pltpu.VMEM((8, ch), F32),
        "ACT": pltpu.VMEM((4, width, ch), BF),
        "POOL": pltpu.VMEM((2, half, ch), BF),
        "GI": pltpu.VMEM((4, c_in, width), BF),
        "GC": pltpu.VMEM((2, half, c_coarse), BF),
        "local_sem": pltpu.SemaphoreType.DMA((24,)),
        "halo_send": pltpu.SemaphoreType.DMA((4, 2)),
        "halo_recv": pltpu.SemaphoreType.DMA((4, 2)),
        "red_send": pltpu.SemaphoreType.DMA((6, z_n + canvas_n)),
        "red_recv": pltpu.SemaphoreType.DMA((6, z_n + canvas_n)),
    }
    for name, (shape, kind) in pieces.items():
        if name == "bias":
            scratch["P_bias"] = pltpu.VMEM((2,) + shape, kind)
            scratch["RA_bias"] = pltpu.VMEM(shape, kind)
        else:
            scratch["P_" + name] = pltpu.VMEM((2, z_n) + shape, kind)
            scratch["RA_" + name] = pltpu.VMEM((z_n,) + shape, kind)
        scratch["Q_" + name] = pltpu.VMEM((z_n,) + shape, kind)
        scratch["RB_" + name] = pltpu.VMEM((z_n,) + shape, kind)
        if fused:
            landing = (canvas_n,) + shape
        else:
            landing = scratch["P_" + name].shape
        outs["RC_" + name] = jax.ShapeDtypeStruct(landing, kind)

    names = list(OPERANDS) + list(outs) + list(scratch)
    sizes = (width, ch, c_in, c_coarse, rows_n, canvas_n, fused)
    results = pl.pallas_call(
        functools.partial(level_kernel, names, sizes),
        out_shape=tuple(outs.values()),
        in_specs=in_specs,
        out_specs=tuple(any_spec for _ in outs),
        scratch_shapes=list(scratch.values()),
        compiler_params=pltpu.CompilerParams(
            collective_id=0, has_side_effects=True, vmem_limit_bytes=VMEM_BYTES
        ),
        name="level",
    )(*(arg[name] for name in OPERANDS))
    held = dict(zip(outs, results))

    if not fused:
        return unfused_tail(held, rows_n, ch, c_in, c_coarse)

    done = {"out_" + name: outs[name] for name in ("activations", "pooled", "grad_inputs", "grad_coarse")}
    for name in ("first", "second", "third", "fourth"):
        shape = pieces[name][0]
        done["out_w_" + name] = jax.ShapeDtypeStruct((3, 3, share, shape[2] // 3), F32)
    done["out_w_up"] = jax.ShapeDtypeStruct((2, 2, share, c_coarse), F32)
    for name in ("first", "second", "up", "third", "fourth"):
        done["out_b_" + name] = jax.ShapeDtypeStruct((1, share), F32)
    big = ("activations", "pooled", "grad_inputs", "grad_coarse")
    finals = pl.pallas_call(
        functools.partial(finish_kernel, list(outs) + list(done) + ["sem"], (ch, share)),
        out_shape=tuple(done.values()),
        in_specs=[any_spec if name in big else vmem_spec for name in outs],
        out_specs=tuple(any_spec if name[4:] in big else vmem_spec for name in done),
        scratch_shapes=[pltpu.SemaphoreType.DMA((4,))],
        name="finish",
    )(*results)
    final = dict(zip(done, finals))
    return ordered(
        {name: final["out_" + name] for name in big},
        {name: final["out_w_" + name] for name in LAYERS},
        {name: final["out_b_" + name].reshape(share) for name in LAYERS},
    )


def ordered(big, weights, biases):
    turned = {name: jnp.swapaxes(value, 2, 3) for name, value in weights.items()}
    pairs = []
    for name in ("first", "second", "up", "third", "fourth"):
        pairs += [turned[name], biases[name]]
    return (
        big["activations"],
        big["pooled"],
        jnp.swapaxes(big["grad_inputs"], 2, 3),
        big["grad_coarse"],
        *pairs,
    )


def unfused_tail(held, rows_n, ch, c_in, c_coarse):
    share = ch // rows_n
    offset = lax.axis_index("rows") * share

    def whole(name):
        parts = held["RC_" + name].astype(F32)
        blocks, piece, lanes = parts.shape[2:]
        parts = jnp.transpose(parts, (2, 1, 0, 3, 4)).reshape(blocks, ch, lanes)
        if name == "up":
            return parts.reshape(2, 2, ch, lanes)
        return jnp.transpose(parts.reshape(3, ch, 3, lanes // 3), (2, 0, 1, 3))

    weights = {name: whole(name) for name in LAYERS}
    weights, biases = lax.psum((weights, held["RC_bias"][0]), ("canvas", "rows"))
    weights = {name: lax.dynamic_slice_in_dim(value, offset, share, 2) for name, value in weights.items()}
    biases = lax.dynamic_slice_in_dim(biases, offset, share, 1)
    places = {"first": 0, "second": 1, "up": 2, "third": 3, "fourth": 4}
    return ordered(held, weights, {name: biases[place] for name, place in places.items()})


def solution(mesh):
    rows_n, canvas_n = mesh.shape["rows"], mesh.shape["canvas"]
    fused = rows_n == 8 and canvas_n == 4
    split = P("canvas", "rows", None, None)
    pairs = (P(None, None, None, "rows"), P("rows"))
    return jax.shard_map(
        functools.partial(on_device, fused, rows_n, canvas_n),
        mesh=mesh,
        in_specs=(split, split, P("canvas", None), P("canvas", None)) + (P(),) * 10 + (split, split),
        out_specs=(split,) * 4 + pairs * 5,
        check_vma=False,
    )
```

profile of v0, /device:TPU:0, one launch (start us, length us, event | category | flops | bytes accessed | tf_op | source)
XLA Modules:
  0.0 84.0 jit_solution(2341160799801590219)
XLA Ops:
  0.7 53.3 %level.1 = (bf16[1,4,384,128]{3,2,1,0:T(8,128)(2,1)}, bf16[1,2,192,128]{3,2,1,0:T(8,128)(2,1)}, bf16[1,4,64,384]{3,2,1,0:T(8,128)(2,1)}, bf16[1,2,192,256]{3,2,1...) custom-call(bf16[1,4,64,384]{3,2,1,0:T(8,128)(2,1)} %bitcast.24, ...), custom_call_target="tpu_custom_call" | custom-call | tf_op jit(solution)/shard_map/level/pallas_call | solution.py:742
  53.9 29.9 %finish.1 = (bf16[1,4,384,128]{3,2,1,0:T(8,128)(2,1)}, bf16[1,2,192,128]{3,2,1,0:T(8,128)(2,1)}, bf16[1,4,64,384]{3,2,1,0:T(8,128)(2,1)}, bf16[1,2,192,256]{3,2,...) custom-call(bf16[1,4,384,128]{3,2,1,0:T(8,128)(2,1)} %get-tuple-elem, ...), custom_call_target="tpu_custom_call" | custom-call | tf_op jit(solution)/shard_map/finish/pallas_call | solution.py:766
where the time goes:
time: 84.1 us; the launch traced here: 84 us
  Pallas kernels  83.2 us (99%)
    pallas_call x1, Pallas kernels, on_device(): pl.pallas_call(functools.partial(level_kernel, names, sizes), out_shape=t...  53.3 us
    pallas_call x1, Pallas kernels, on_device(): pl.pallas_call(functools.partial(finish_kernel, list(outs) + list(done) +...  29.9 us

commit v1 on v0

--- a/solution.py
+++ b/solution.py
@@ -1,4 +1,5 @@
 import functools
+import types
 
 import jax
 import jax.numpy as jnp
@@ -12,25 +13,10 @@
 F32 = jnp.float32
 VMEM_BYTES = 58 * 2**20
 
-OPERANDS = (
-    "inputs",
-    "coarse",
-    "row_cuts",
-    "col_cuts",
-    "w_first",
-    "b_first",
-    "w_second",
-    "b_second",
-    "w_up",
-    "b_up",
-    "w_third",
-    "b_third",
-    "w_fourth",
-    "b_fourth",
-    "cot_out",
-    "cot_pool",
-)
-LAYERS = ("fourth", "third", "up", "second", "first")
+FIRST, SECOND, UP, THIRD, FOURTH, BIAS = "first", "second", "up", "third", "fourth", "bias"
+LAYERS = (FOURTH, THIRD, UP, SECOND, FIRST)
+ORDER = (FIRST, SECOND, UP, THIRD, FOURTH)
+BIG = ("activations", "pooled", "grad_inputs", "grad_coarse")
 
 
 def dot_nn(a, b):
@@ -52,7 +38,7 @@
 
 
 def level_kernel(names, sizes, *refs):
-    ref = dict(zip(names, refs))
+    ref = types.SimpleNamespace(**dict(zip(names, refs)))
     width, ch, c_in, c_coarse, rows_n, canvas_n, fused = sizes
     half = width // 2
     c = lax.axis_index("canvas")
@@ -75,7 +61,7 @@
         for step in range(1, canvas_n):
             greet((lax.rem(c + step, canvas_n), r))
 
-    local_sem = ref["local_sem"]
+    local_sem = ref.local_sem
     used = [0]
 
     def fetch(src, dst):
@@ -84,46 +70,43 @@
         copy.start()
         return copy
 
-    X, CO = ref["X"], ref["CO"]
-    in_x = fetch(ref["inputs"].at[0], X.at[pl.ds(4, 4)])
-    in_w1 = fetch(ref["w_first"], ref["KB1"].at[pl.ds(1, 3)])
-    in_co = fetch(ref["coarse"].at[0], CO.at[pl.ds(1, 2)])
+    X, CO = ref.X, ref.CO
+    in_x = fetch(ref.inputs.at[0], X.at[pl.ds(4, 4)])
+    in_w1 = fetch(ref.w_first, ref.KB1.at[pl.ds(1, 3)])
+    in_co = fetch(ref.coarse.at[0], CO.at[pl.ds(1, 2)])
     in_up = [
-        fetch(ref["w_up"].at[a, b], ref["WU"].at[:, pl.ds((2 * a + b) * ch, ch)])
+        fetch(ref.w_up.at[a, b], ref.WU.at[:, pl.ds((2 * a + b) * ch, ch)])
         for a in (0, 1)
         for b in (0, 1)
     ]
-    in_w2 = fetch(ref["w_second"], ref["KB2"].at[pl.ds(1, 3)])
-    in_w3 = fetch(ref["w_third"], ref["KB3"].at[pl.ds(1, 3)])
-    in_w4 = fetch(ref["w_fourth"], ref["KB4"].at[pl.ds(1, 3)])
-    in_cot = fetch(ref["cot_out"].at[0], ref["COT"])
-    in_cp = fetch(ref["cot_pool"].at[0], ref["CP"])
+    in_w2 = fetch(ref.w_second, ref.KB2.at[pl.ds(1, 3)])
+    in_w3 = fetch(ref.w_third, ref.KB3.at[pl.ds(1, 3)])
+    in_w4 = fetch(ref.w_fourth, ref.KB4.at[pl.ds(1, 3)])
+    in_cot = fetch(ref.cot_out.at[0], ref.COT)
+    in_cp = fetch(ref.cot_pool.at[0], ref.CP)
 
     first, total_rows = r * 4, rows_n * 4
 
     def link(h):
         row = first + h
         inside = jnp.logical_and(row > 0, row < total_rows)
-        cut = ref["row_cuts"][0, jnp.clip(row, 0, total_rows - 1)]
+        cut = ref.row_cuts[0, jnp.clip(row, 0, total_rows - 1)]
         return jnp.where(inside, 1 - cut, 0)
 
-    open_row = 1.0 - ref["col_cuts"][...].astype(F32)
+    open_row = 1.0 - ref.col_cuts[...].astype(F32)
     open_row = jnp.where(lax.broadcasted_iota(jnp.int32, (1, width), 1) > 0, open_row, 0.0)
     left_gate = jnp.broadcast_to(open_row, (128, width))
     right_gate = pltpu.roll(left_gate, width - 1, 1)
-    GL, GR = ref["GL"], ref["GR"]
+    GL, GR = ref.GL, ref.GR
     GL[...] = left_gate.T
     GR[...] = right_gate.T
     left_row, right_row = left_gate[:c_in], right_gate[:c_in]
 
-    for name in ("KB1", "KB2", "KB3", "KB4"):
-        ref[name][0] = jnp.zeros(ref[name].shape[1:], BF)
-    for name in ("KT1", "KT2", "KT4", "VA", "VJ", "VC"):
-        ref[name][0] = jnp.zeros(ref[name].shape[1:], BF)
-    ref["KT3"][0] = jnp.zeros(ref["KT3"].shape[1:], BF)
+    for bank in (ref.KB1, ref.KB2, ref.KB3, ref.KB4, ref.KT1, ref.KT2, ref.KT3, ref.KT4, ref.VA, ref.VJ, ref.VC):
+        bank[0] = jnp.zeros(bank.shape[1:], BF)
     X[12] = jnp.zeros(X.shape[1:], BF)
 
-    halo_send, halo_recv = ref["halo_send"], ref["halo_recv"]
+    halo_send, halo_recv = ref.halo_send, ref.halo_recv
 
     def remote(src, dst, send, recv, device):
         return pltpu.make_async_remote_copy(
@@ -147,9 +130,9 @@
         pl.when(has_up)(lambda: pair[0].wait_send())
         pl.when(has_down)(lambda: pair[1].wait_send())
 
-    G4, G2 = ref["G4"], ref["G2"]
-    x_halo = pair_exchange(0, ref["inputs"].at[0], X.at[pl.ds(8, 4)], ref["inputs"].at[0], X.at[pl.ds(0, 4)])
-    co_halo = pair_exchange(1, ref["coarse"].at[0, 0], CO.at[3], ref["coarse"].at[0, 1], CO.at[0])
+    G4, G2 = ref.G4, ref.G2
+    x_halo = pair_exchange(0, ref.inputs.at[0], X.at[pl.ds(8, 4)], ref.inputs.at[0], X.at[pl.ds(0, 4)])
+    co_halo = pair_exchange(1, ref.coarse.at[0, 0], CO.at[3], ref.coarse.at[0, 1], CO.at[0])
     g4_halo = pair_exchange(2, G4.at[pl.ds(2, 2)], G4.at[pl.ds(6, 2)], G4.at[pl.ds(4, 2)], G4.at[pl.ds(0, 2)])
     g2_halo = pair_exchange(3, G2.at[pl.ds(2, 2)], G2.at[pl.ds(6, 2)], G2.at[pl.ds(4, 2)], G2.at[pl.ds(0, 2)])
 
@@ -213,13 +196,13 @@
         return dot_nt(band, back_weights(bank, h))
 
     def bias(name):
-        return ref[name][...].astype(F32).reshape(1, ch)
-
-    V3X, V3A, V3J, V3C = ref["V3X"], ref["V3A"], ref["V3J"], ref["V3C"]
-    VA, VJ, VC = ref["VA"], ref["VJ"], ref["VC"]
-    S1, S2, S3 = ref["S1"], ref["S2"], ref["S3"]
-    KB1, KB2, KB3, KB4 = ref["KB1"], ref["KB2"], ref["KB3"], ref["KB4"]
-    KT1, KT2, KT3, KT4 = ref["KT1"], ref["KT2"], ref["KT3"], ref["KT4"]
+        return getattr(ref, name)[...].astype(F32).reshape(1, ch)
+
+    V3X, V3A, V3J, V3C = ref.V3X, ref.V3A, ref.V3J, ref.V3C
+    VA, VJ, VC = ref.VA, ref.VJ, ref.VC
+    S1, S2, S3 = ref.S1, ref.S2, ref.S3
+    KB1, KB2, KB3, KB4 = ref.KB1, ref.KB2, ref.KB3, ref.KB4
+    KT1, KT2, KT3, KT4 = ref.KT1, ref.KT2, ref.KT3, ref.KT4
 
     def widen_input(row):
         value = X[row].astype(F32)
@@ -228,7 +211,7 @@
         V3X[row, 2 * c_in : 3 * c_in] = (pltpu.roll(value, width - 1, 1) * right_row).astype(BF)
 
     b_first, b_second, b_up, b_third, b_fourth = (
-        bias("b_" + name) for name in ("first", "second", "up", "third", "fourth")
+        bias("b_" + name) for name in ORDER
     )
 
     def first_pair(h):
@@ -255,8 +238,8 @@
         widen_input(row)
     first_pair(1)
 
-    SA, SB = ref["SA"], ref["SB"]
-    WU = ref["WU"]
+    SA, SB = ref.SA, ref.SB
+    WU = ref.WU
 
     def up_rows(i):
         fine = dot_nn(CO[i], WU[...])
@@ -292,7 +275,7 @@
     for h in (-1, 3, -3, 5):
         first_pair(h)
 
-    pooled_buf = ref["POOL"]
+    pooled_buf = ref.POOL
 
     def second_pair(h):
         both = conv_pair(V3A, h + 3, KB2, h)
@@ -313,7 +296,7 @@
 
     for h in (0, 2, -2, 4):
         second_pair(h)
-    out_pool = fetch(pooled_buf, ref["pooled"].at[0])
+    out_pool = fetch(pooled_buf, ref.pooled.at[0])
 
     receive(co_halo)
     up_rows(0)
@@ -330,9 +313,9 @@
     for h in (1, -1, 3):
         third_pair(h)
 
-    G34, G33, G32, G31 = ref["G34"], ref["G33"], ref["G32"], ref["G31"]
-    DB = ref["DB"]
-    COT, ACT = ref["COT"], ref["ACT"]
+    G34, G33, G32, G31 = ref.G34, ref.G33, ref.G32, ref.G31
+    DB = ref.DB
+    COT, ACT = ref.COT, ref.ACT
     in_cot.wait()
     in_cp.wait()
     sums = {}
@@ -349,24 +332,24 @@
             g = (COT[h + j].astype(F32) * slope).astype(BF)
             G4[h + j + 2] = g
             g = g.astype(F32)
-            add_sum("fourth", g)
+            add_sum(FOURTH, g)
             put_wide(G34, h + j + 2, g)
 
     fourth_pair(0)
     pl.when(has_up)(lambda: g4_halo[0].start())
     fourth_pair(2)
     pl.when(has_down)(lambda: g4_halo[1].start())
-    out_act = fetch(ACT, ref["activations"].at[0])
+    out_act = fetch(ACT, ref.activations.at[0])
 
     partner = (c, r + 1 - 2 * k)
 
     class Reduction:
         def __init__(self, index, name):
             self.index, self.name = index, name
-            self.part, self.twin = ref["P_" + name], ref["RA_" + name]
-            self.sums, self.along = ref["Q_" + name], ref["RB_" + name]
-            self.slots = ref["RC_" + name]
-            self.send, self.recv = ref["red_send"], ref["red_recv"]
+            self.part, self.twin = getattr(ref, "P_" + name), getattr(ref, "RA_" + name)
+            self.sums, self.along = getattr(ref, "Q_" + name), getattr(ref, "RB_" + name)
+            self.slots = getattr(ref, "RC_" + name)
+            self.send, self.recv = ref.red_send, ref.red_recv
 
         def copies_z(self):
             found = []
@@ -434,13 +417,13 @@
                 copy.wait()
             self.own.wait()
 
-    red = {name: Reduction(index, name) for index, name in enumerate(LAYERS + ("bias",))}
+    red = {name: Reduction(index, name) for index, name in enumerate(LAYERS + (BIAS,))}
 
     def put_parts(name, value):
-        part = ref["P_" + name]
+        part = getattr(ref, "P_" + name)
         blocks, share = part.shape[2], part.shape[3]
         for block in range(blocks):
-            place = block if name == "up" else blocks - 1 - block
+            place = block if name == UP else blocks - 1 - block
             for owner in range(8):
                 lo = block * ch + owner * share
                 part[owner % 2, owner // 2, place] = value[lo : lo + share].astype(BF)
@@ -463,27 +446,27 @@
         for j in (0, 1):
             g = (both[:, j * ch : (j + 1) * ch] * S3[h + j + 1]).astype(BF).astype(F32)
             if 0 <= h + j < 4:
-                add_sum("third", g)
+                add_sum(THIRD, g)
             put_wide(G33, h + j + 1, g)
 
-    put_parts("fourth", weight_grad(G34, 2, VC, 2))
-    red["fourth"].start_core()
+    put_parts(FOURTH, weight_grad(G34, 2, VC, 2))
+    red[FOURTH].start_core()
     third_back(1)
     receive(g4_halo)
     for row in (0, 1, 6, 7):
         load_wide(G34, row, G4[row])
     third_back(-1)
     third_back(3)
-    red["fourth"].start_z()
-
-    GB, CP = ref["GB"], ref["CP"]
+    red[FOURTH].start_z()
+
+    GB, CP = ref.GB, ref.CP
 
     def joined_back(h):
         band = jnp.concatenate([G33[h + 1 + d] for d in (-1, 0, 1)], axis=1)
         weights = jnp.concatenate([KT3[link(h)], KT3[2], KT3[link(h + 1) * 3]], axis=1)
         d_joined = dot_nt(band, weights)
         g_up = d_joined[:, :ch].astype(BF).astype(F32)
-        add_sum("up", g_up)
+        add_sum(UP, g_up)
         a = h % 2
         SA[a] = g_up
         for b in (0, 1):
@@ -496,7 +479,7 @@
         g = ((d_joined[:, ch:] + SB[...]) * S2[h]).astype(BF)
         G2[h + 2] = g
         g = g.astype(F32)
-        add_sum("second", g)
+        add_sum(SECOND, g)
         put_wide(G32, h + 2, g)
 
     joined_back(0)
@@ -506,23 +489,23 @@
     joined_back(3)
     pl.when(has_down)(lambda: g2_halo[1].start())
 
-    put_parts("third", weight_grad(G33, 1, VJ, 3))
-    red["third"].start_core()
-    red["fourth"].start_canvas()
+    put_parts(THIRD, weight_grad(G33, 1, VJ, 3))
+    red[THIRD].start_core()
+    red[FOURTH].start_canvas()
     bands = GB[...].reshape(2 * half, 4 * ch)
-    put_parts("up", dot_tn(bands, CO[1:3].reshape(2 * half, c_coarse)))
-    red["up"].start_core()
-    red["third"].start_z()
-    put_parts("second", weight_grad(G32, 2, VA, 4))
-    red["second"].start_core()
-    red["up"].start_z()
+    put_parts(UP, dot_tn(bands, CO[1:3].reshape(2 * half, c_coarse)))
+    red[UP].start_core()
+    red[THIRD].start_z()
+    put_parts(SECOND, weight_grad(G32, 2, VA, 4))
+    red[SECOND].start_core()
+    red[UP].start_z()
 
     def first_back(h):
         both = back_pair(G32, h + 2, KT2, h)
         for j in (0, 1):
             g = (both[:, j * ch : (j + 1) * ch] * S1[h + j + 3]).astype(BF).astype(F32)
             if 0 <= h + j < 4:
-                add_sum("first", g)
+                add_sum(FIRST, g)
             put_wide(G31, h + j + 1, g)
 
     first_back(1)
@@ -542,19 +525,19 @@
         ],
         axis=1,
     )
-    put_parts("first", dot_nn(stacked, G31[1:5].reshape(4 * width, 3 * ch)).T)
-    red["first"].start_core()
-    for place, name in enumerate(("first", "second", "up", "third", "fourth")):
+    put_parts(FIRST, dot_nn(stacked, G31[1:5].reshape(4 * width, 3 * ch)).T)
+    red[FIRST].start_core()
+    for place, name in enumerate(ORDER):
         DB[place : place + 1] = jnp.sum(sums[name], axis=0, keepdims=True)
     if fused:
-        ref["P_bias"][0] = DB[...]
-        ref["P_bias"][1] = DB[...]
+        ref.P_bias[0] = DB[...]
+        ref.P_bias[1] = DB[...]
     else:
-        ref["P_bias"][0] = DB[...]
-    red["bias"].start_core()
-    red["second"].start_z()
-
-    GI = ref["GI"]
+        ref.P_bias[0] = DB[...]
+    red[BIAS].start_core()
+    red[SECOND].start_z()
+
+    GI = ref.GI
 
     def input_back(h):
         weights = back_weights(KT1, h)
@@ -563,20 +546,20 @@
         GI[h] = both[:c_in]
         GI[h + 1] = both[c_in:]
 
-    red["first"].start_z()
+    red[FIRST].start_z()
     input_back(0)
     input_back(2)
-    out_gi = fetch(GI, ref["grad_inputs"].at[0])
-    GC = ref["GC"]
+    out_gi = fetch(GI, ref.grad_inputs.at[0])
+    GC = ref.GC
     for i in (0, 1):
         GC[i] = dot_nt(GB[i], WU[...]).astype(BF)
-    out_gc = fetch(GC, ref["grad_coarse"].at[0])
-    red["third"].start_canvas()
-    red["up"].start_canvas()
-    red["second"].start_canvas()
+    out_gc = fetch(GC, ref.grad_coarse.at[0])
+    red[THIRD].start_canvas()
+    red[UP].start_canvas()
+    red[SECOND].start_canvas()
 
     if fused:
-        bias_red = red["bias"]
+        bias_red = red[BIAS]
         bias_red.core.wait_recv()
         bias_red.sums[z] = bias_red.part[k] + bias_red.twin[...]
         bias_red.along_copies = []
@@ -590,10 +573,10 @@
             )
         for copy in bias_red.along_copies:
             copy.start()
-    red["first"].start_canvas()
-    red["bias"].start_canvas()
-
-    for name in LAYERS + ("bias",):
+    red[FIRST].start_canvas()
+    red[BIAS].start_canvas()
+
+    for name in LAYERS + (BIAS,):
         red[name].finish()
     for pair in (x_halo, co_halo, g4_halo, g2_halo):
         sent(pair)
@@ -602,14 +585,17 @@
 
 
 def finish_kernel(names, sizes, *refs):
-    ref = dict(zip(names, refs))
+    ref = types.SimpleNamespace(**dict(zip(names, refs)))
+    ref.held, ref.sem = refs[-5:-1], refs[-1]
     ch, share = sizes
     r = lax.axis_index("rows")
     copies = []
-    for place, name in enumerate(("activations", "pooled", "grad_inputs", "grad_coarse")):
-        copy = pltpu.make_async_copy(ref[name], ref["out_" + name], ref["sem"].at[place])
-        copy.start()
-        copies.append(copy)
+    for place, name in enumerate(BIG):
+        held = ref.held[place]
+        enter = pltpu.make_async_copy(getattr(ref, name), held, ref.sem.at[0, place])
+        leave = pltpu.make_async_copy(held, getattr(ref, "out_" + name), ref.sem.at[1, place])
+        enter.start()
+        copies.append((enter, leave))
 
     def total(slots):
         value = slots[0].astype(F32)
@@ -617,25 +603,65 @@
             value = value + slots[place].astype(F32)
         return value
 
-    for name in ("first", "second", "third", "fourth"):
-        value = total(ref["RC_" + name])
-        out = ref["out_w_" + name]
+    for name in (FIRST, SECOND, THIRD, FOURTH):
+        value = total(getattr(ref, "RC_" + name))
+        out = getattr(ref, "out_w_" + name)
         part = out.shape[3]
         for row_tap in range(3):
             out[row_tap] = value[:, :, row_tap * part : (row_tap + 1) * part]
-    value = total(ref["RC_up"])
+    value = total(ref.RC_up)
     for a in (0, 1):
         for b in (0, 1):
-            ref["out_w_up"][a, b] = value[2 * a + b]
-    sums = pltpu.roll(total(ref["RC_bias"]), lax.rem(ch - r * share, ch), 1)
-    for place, name in enumerate(("first", "second", "up", "third", "fourth")):
-        ref["out_b_" + name][...] = sums[place : place + 1, :share]
-    for copy in copies:
-        copy.wait()
-
-
-def on_device(fused, rows_n, canvas_n, *args):
-    arg = dict(zip(OPERANDS, args))
+            ref.out_w_up[a, b] = value[2 * a + b]
+    sums = pltpu.roll(total(ref.RC_bias), lax.rem(ch - r * share, ch), 1)
+    for place, name in enumerate(ORDER):
+        getattr(ref, "out_b_" + name)[...] = sums[place : place + 1, :share]
+    for enter, leave in copies:
+        enter.wait()
+        leave.start()
+    for enter, leave in copies:
+        leave.wait()
+
+
+def on_device(
+    fused,
+    rows_n,
+    canvas_n,
+    inputs,
+    coarse,
+    row_cuts,
+    col_cuts,
+    w_first,
+    b_first,
+    w_second,
+    b_second,
+    w_up,
+    b_up,
+    w_third,
+    b_third,
+    w_fourth,
+    b_fourth,
+    cot_out,
+    cot_pool,
+):
+    arg = dict(
+        inputs=inputs,
+        coarse=coarse,
+        row_cuts=row_cuts,
+        col_cuts=col_cuts,
+        w_first=w_first,
+        b_first=b_first,
+        w_second=w_second,
+        b_second=b_second,
+        w_up=w_up,
+        b_up=b_up,
+        w_third=w_third,
+        b_third=b_third,
+        w_fourth=w_fourth,
+        b_fourth=b_fourth,
+        cot_out=cot_out,
+        cot_pool=cot_pool,
+    )
     _, length, width, c_in = arg["inputs"].shape
     ch = arg["w_first"].shape[3]
     c_coarse = arg["coarse"].shape[3]
@@ -646,13 +672,14 @@
     arg["w_second"] = arg["w_second"].reshape(3, 3 * ch, ch)
     arg["w_third"] = arg["w_third"].reshape(3, 6 * ch, ch)
     arg["w_fourth"] = arg["w_fourth"].reshape(3, 3 * ch, ch)
-    for name in ("b_first", "b_second", "b_up", "b_third", "b_fourth"):
+    for name in ORDER:
+        name = "b_" + name
         arg[name] = arg[name].reshape(1, ch)
 
     any_spec = pl.BlockSpec(memory_space=pl.ANY)
     vmem_spec = pl.BlockSpec(memory_space=pltpu.VMEM)
     in_specs = []
-    for name in OPERANDS:
+    for name in arg:
         if name == "row_cuts":
             in_specs.append(pl.BlockSpec(memory_space=pltpu.SMEM))
         elif name == "col_cuts" or name.startswith("b_"):
@@ -662,68 +689,68 @@
 
     owners, z_n = 8, 4
     share = ch // owners
-    pieces = {
-        "fourth": ((3, share, 3 * ch), BF),
-        "third": ((3, share, 6 * ch), BF),
-        "up": ((4, share, c_coarse), BF),
-        "second": ((3, share, 3 * ch), BF),
-        "first": ((3, share, 3 * c_in), BF),
-        "bias": ((8, ch), F32),
-    }
-    outs = {
-        "activations": jax.ShapeDtypeStruct((1, 4, width, ch), BF),
-        "pooled": jax.ShapeDtypeStruct((1, 2, half, ch), BF),
-        "grad_inputs": jax.ShapeDtypeStruct((1, 4, c_in, width), BF),
-        "grad_coarse": jax.ShapeDtypeStruct((1, 2, half, c_coarse), BF),
-    }
-    scratch = {
-        "X": pltpu.VMEM((13, c_in, width), BF),
-        "CO": pltpu.VMEM((4, half, c_coarse), BF),
-        "COT": pltpu.VMEM((4, width, ch), BF),
-        "CP": pltpu.VMEM((2, half, ch), BF),
-        "WU": pltpu.VMEM((c_coarse, 4 * ch), BF),
-        "GL": pltpu.VMEM((width, ch), F32),
-        "GR": pltpu.VMEM((width, ch), F32),
-        "KB1": pltpu.VMEM((4, 3 * c_in, ch), BF),
-        "KB2": pltpu.VMEM((4, 3 * ch, ch), BF),
-        "KB3": pltpu.VMEM((4, 6 * ch, ch), BF),
-        "KB4": pltpu.VMEM((4, 3 * ch, ch), BF),
-        "KT1": pltpu.VMEM((4, c_in, 3 * ch), BF),
-        "KT2": pltpu.VMEM((4, ch, 3 * ch), BF),
-        "KT3": pltpu.VMEM((4, 2 * ch, 3 * ch), BF),
-        "KT4": pltpu.VMEM((4, ch, 3 * ch), BF),
-        "V3X": pltpu.VMEM((12, 3 * c_in, width), BF),
-        "V3A": pltpu.VMEM((10, width, 3 * ch), BF),
-        "V3J": pltpu.VMEM((8, width, 6 * ch), BF),
-        "V3C": pltpu.VMEM((6, width, 3 * ch), BF),
-        "VA": pltpu.VMEM((11, width, ch), BF),
-        "VJ": pltpu.VMEM((9, width, 2 * ch), BF),
-        "VC": pltpu.VMEM((7, width, ch), BF),
-        "S1": pltpu.VMEM((10, width, ch), F32),
-        "S2": pltpu.VMEM((4, width, ch), F32),
-        "S3": pltpu.VMEM((6, width, ch), F32),
-        "G4": pltpu.VMEM((8, width, ch), BF),
-        "G2": pltpu.VMEM((8, width, ch), BF),
-        "G34": pltpu.VMEM((8, width, 3 * ch), BF),
-        "G33": pltpu.VMEM((6, width, 3 * ch), BF),
-        "G32": pltpu.VMEM((8, width, 3 * ch), BF),
-        "G31": pltpu.VMEM((6, width, 3 * ch), BF),
-        "GB": pltpu.VMEM((2, half, 4 * ch), BF),
-        "SA": pltpu.VMEM((2, width, ch), F32),
-        "SB": pltpu.VMEM((width, ch), F32),
-        "DB": pltpu.VMEM((8, ch), F32),
-        "ACT": pltpu.VMEM((4, width, ch), BF),
-        "POOL": pltpu.VMEM((2, half, ch), BF),
-        "GI": pltpu.VMEM((4, c_in, width), BF),
-        "GC": pltpu.VMEM((2, half, c_coarse), BF),
-        "local_sem": pltpu.SemaphoreType.DMA((24,)),
-        "halo_send": pltpu.SemaphoreType.DMA((4, 2)),
-        "halo_recv": pltpu.SemaphoreType.DMA((4, 2)),
-        "red_send": pltpu.SemaphoreType.DMA((6, z_n + canvas_n)),
-        "red_recv": pltpu.SemaphoreType.DMA((6, z_n + canvas_n)),
-    }
+    pieces = dict(
+        fourth=((3, share, 3 * ch), BF),
+        third=((3, share, 6 * ch), BF),
+        up=((4, share, c_coarse), BF),
+        second=((3, share, 3 * ch), BF),
+        first=((3, share, 3 * c_in), BF),
+        bias=((8, ch), F32),
+    )
+    outs = dict(
+        activations=jax.ShapeDtypeStruct((1, 4, width, ch), BF),
+        pooled=jax.ShapeDtypeStruct((1, 2, half, ch), BF),
+        grad_inputs=jax.ShapeDtypeStruct((1, 4, c_in, width), BF),
+        grad_coarse=jax.ShapeDtypeStruct((1, 2, half, c_coarse), BF),
+    )
+    scratch = dict(
+        X=pltpu.VMEM((13, c_in, width), BF),
+        CO=pltpu.VMEM((4, half, c_coarse), BF),
+        COT=pltpu.VMEM((4, width, ch), BF),
+        CP=pltpu.VMEM((2, half, ch), BF),
+        WU=pltpu.VMEM((c_coarse, 4 * ch), BF),
+        GL=pltpu.VMEM((width, ch), F32),
+        GR=pltpu.VMEM((width, ch), F32),
+        KB1=pltpu.VMEM((4, 3 * c_in, ch), BF),
+        KB2=pltpu.VMEM((4, 3 * ch, ch), BF),
+        KB3=pltpu.VMEM((4, 6 * ch, ch), BF),
+        KB4=pltpu.VMEM((4, 3 * ch, ch), BF),
+        KT1=pltpu.VMEM((4, c_in, 3 * ch), BF),
+        KT2=pltpu.VMEM((4, ch, 3 * ch), BF),
+        KT3=pltpu.VMEM((4, 2 * ch, 3 * ch), BF),
+        KT4=pltpu.VMEM((4, ch, 3 * ch), BF),
+        V3X=pltpu.VMEM((12, 3 * c_in, width), BF),
+        V3A=pltpu.VMEM((10, width, 3 * ch), BF),
+        V3J=pltpu.VMEM((8, width, 6 * ch), BF),
+        V3C=pltpu.VMEM((6, width, 3 * ch), BF),
+        VA=pltpu.VMEM((11, width, ch), BF),
+        VJ=pltpu.VMEM((9, width, 2 * ch), BF),
+        VC=pltpu.VMEM((7, width, ch), BF),
+        S1=pltpu.VMEM((10, width, ch), F32),
+        S2=pltpu.VMEM((4, width, ch), F32),
+        S3=pltpu.VMEM((6, width, ch), F32),
+        G4=pltpu.VMEM((8, width, ch), BF),
+        G2=pltpu.VMEM((8, width, ch), BF),
+        G34=pltpu.VMEM((8, width, 3 * ch), BF),
+        G33=pltpu.VMEM((6, width, 3 * ch), BF),
+        G32=pltpu.VMEM((8, width, 3 * ch), BF),
+        G31=pltpu.VMEM((6, width, 3 * ch), BF),
+        GB=pltpu.VMEM((2, half, 4 * ch), BF),
+        SA=pltpu.VMEM((2, width, ch), F32),
+        SB=pltpu.VMEM((width, ch), F32),
+        DB=pltpu.VMEM((8, ch), F32),
+        ACT=pltpu.VMEM((4, width, ch), BF),
+        POOL=pltpu.VMEM((2, half, ch), BF),
+        GI=pltpu.VMEM((4, c_in, width), BF),
+        GC=pltpu.VMEM((2, half, c_coarse), BF),
+        local_sem=pltpu.SemaphoreType.DMA((24,)),
+        halo_send=pltpu.SemaphoreType.DMA((4, 2)),
+        halo_recv=pltpu.SemaphoreType.DMA((4, 2)),
+        red_send=pltpu.SemaphoreType.DMA((6, z_n + canvas_n)),
+        red_recv=pltpu.SemaphoreType.DMA((6, z_n + canvas_n)),
+    )
     for name, (shape, kind) in pieces.items():
-        if name == "bias":
+        if name == BIAS:
             scratch["P_bias"] = pltpu.VMEM((2,) + shape, kind)
             scratch["RA_bias"] = pltpu.VMEM(shape, kind)
         else:
@@ -737,7 +764,7 @@
             landing = scratch["P_" + name].shape
         outs["RC_" + name] = jax.ShapeDtypeStruct(landing, kind)
 
-    names = list(OPERANDS) + list(outs) + list(scratch)
+    names = list(arg) + list(outs) + list(scratch)
     sizes = (width, ch, c_in, c_coarse, rows_n, canvas_n, fused)
     results = pl.pallas_call(
         functools.partial(level_kernel, names, sizes),
@@ -749,31 +776,30 @@
             collective_id=0, has_side_effects=True, vmem_limit_bytes=VMEM_BYTES
         ),
         name="level",
-    )(*(arg[name] for name in OPERANDS))
+    )(*(arg[name] for name in arg))
     held = dict(zip(outs, results))
 
     if not fused:
         return unfused_tail(held, rows_n, ch, c_in, c_coarse)
 
-    done = {"out_" + name: outs[name] for name in ("activations", "pooled", "grad_inputs", "grad_coarse")}
-    for name in ("first", "second", "third", "fourth"):
+    done = {"out_" + name: outs[name] for name in BIG}
+    for name in (FIRST, SECOND, THIRD, FOURTH):
         shape = pieces[name][0]
         done["out_w_" + name] = jax.ShapeDtypeStruct((3, 3, share, shape[2] // 3), F32)
     done["out_w_up"] = jax.ShapeDtypeStruct((2, 2, share, c_coarse), F32)
-    for name in ("first", "second", "up", "third", "fourth"):
+    for name in ORDER:
         done["out_b_" + name] = jax.ShapeDtypeStruct((1, share), F32)
-    big = ("activations", "pooled", "grad_inputs", "grad_coarse")
     finals = pl.pallas_call(
-        functools.partial(finish_kernel, list(outs) + list(done) + ["sem"], (ch, share)),
+        functools.partial(finish_kernel, list(outs) + list(done), (ch, share)),
         out_shape=tuple(done.values()),
-        in_specs=[any_spec if name in big else vmem_spec for name in outs],
-        out_specs=tuple(any_spec if name[4:] in big else vmem_spec for name in done),
-        scratch_shapes=[pltpu.SemaphoreType.DMA((4,))],
+        in_specs=[any_spec if name in BIG else vmem_spec for name in outs],
+        out_specs=tuple(any_spec if name[4:] in BIG else vmem_spec for name in done),
+        scratch_shapes=[pltpu.VMEM(outs[name].shape, BF) for name in BIG] + [pltpu.SemaphoreType.DMA((2, 4))],
         name="finish",
     )(*results)
     final = dict(zip(done, finals))
     return ordered(
-        {name: final["out_" + name] for name in big},
+        {name: final["out_" + name] for name in BIG},
         {name: final["out_w_" + name] for name in LAYERS},
         {name: final["out_b_" + name].reshape(share) for name in LAYERS},
     )
@@ -782,7 +808,7 @@
 def ordered(big, weights, biases):
     turned = {name: jnp.swapaxes(value, 2, 3) for name, value in weights.items()}
     pairs = []
-    for name in ("first", "second", "up", "third", "fourth"):
+    for name in ORDER:
         pairs += [turned[name], biases[name]]
     return (
         big["activations"],
@@ -801,7 +827,7 @@
         parts = held["RC_" + name].astype(F32)
         blocks, piece, lanes = parts.shape[2:]
         parts = jnp.transpose(parts, (2, 1, 0, 3, 4)).reshape(blocks, ch, lanes)
-        if name == "up":
+        if name == UP:
             return parts.reshape(2, 2, ch, lanes)
         return jnp.transpose(parts.reshape(3, ch, 3, lanes // 3), (2, 0, 1, 3))
 
@@ -809,7 +835,7 @@
     weights, biases = lax.psum((weights, held["RC_bias"][0]), ("canvas", "rows"))
     weights = {name: lax.dynamic_slice_in_dim(value, offset, share, 2) for name, value in weights.items()}
     biases = lax.dynamic_slice_in_dim(biases, offset, share, 1)
-    places = {"first": 0, "second": 1, "up": 2, "third": 3, "fourth": 4}
+    places = {FIRST: 0, SECOND: 1, UP: 2, THIRD: 3, FOURTH: 4}
     return ordered(held, weights, {name: biases[place] for name, place in places.items()})
 
 

time: 84.1 us -> 58.2 us (0.69)
  Pallas kernels: 83.2 us -> 57.2 us
    pallas_call x1, Pallas kernels: 29.9 us -> 3.93 us  [on_device(): pl.pallas_call(functools.partial(finish_kernel, list(outs) + list(done),...]
where the time goes in v1:
time: 58.2 us; the launch traced here: 58 us
  Pallas kernels  57.2 us (98%)
  between operations  0.82 us (1%)
    pallas_call x1, Pallas kernels, on_device(): pl.pallas_call(functools.partial(level_kernel, names, sizes), out_shape=t...  53.3 us
    pallas_call x1, Pallas kernels, on_device(): pl.pallas_call(functools.partial(finish_kernel, list(outs) + list(done),...  3.93 us

profile of v1, /device:TPU:0, one launch (start us, length us, event | category | flops | bytes accessed | tf_op | source)
XLA Modules:
  0.0 58.0 jit_solution(2711387700008850047)
XLA Ops:
  0.7 53.3 %level.1 = (bf16[1,4,384,128]{3,2,1,0:T(8,128)(2,1)}, bf16[1,2,192,128]{3,2,1,0:T(8,128)(2,1)}, bf16[1,4,64,384]{3,2,1,0:T(8,128)(2,1)}, bf16[1,2,192,256]{3,2,1...) custom-call(bf16[1,4,64,384]{3,2,1,0:T(8,128)(2,1)} %bitcast.24, ...), custom_call_target="tpu_custom_call" | custom-call | tf_op jit(solution)/shard_map/level/pallas_call | solution.py:769
  53.9 3.9 %finish.1 = (bf16[1,4,384,128]{3,2,1,0:T(8,128)(2,1)}, bf16[1,2,192,128]{3,2,1,0:T(8,128)(2,1)}, bf16[1,4,64,384]{3,2,1,0:T(8,128)(2,1)}, bf16[1,2,192,256]{3,2,...) custom-call(bf16[1,4,384,128]{3,2,1,0:T(8,128)(2,1)} %get-tuple-elem, ...), custom_call_target="tpu_custom_call" | custom-call | tf_op jit(solution)/shard_map/finish/pallas_call | solution.py:792

commit v2 on v1

--- a/solution.py
+++ b/solution.py
@@ -13,8 +13,9 @@
 F32 = jnp.float32
 VMEM_BYTES = 58 * 2**20
 
-FIRST, SECOND, UP, THIRD, FOURTH, BIAS = "first", "second", "up", "third", "fourth", "bias"
+FIRST, SECOND, UP, THIRD, FOURTH = "first", "second", "up", "third", "fourth"
 LAYERS = (FOURTH, THIRD, UP, SECOND, FIRST)
+WIDE = (FOURTH, THIRD)
 ORDER = (FIRST, SECOND, UP, THIRD, FOURTH)
 BIG = ("activations", "pooled", "grad_inputs", "grad_coarse")
 
@@ -105,6 +106,8 @@
     for bank in (ref.KB1, ref.KB2, ref.KB3, ref.KB4, ref.KT1, ref.KT2, ref.KT3, ref.KT4, ref.VA, ref.VJ, ref.VC):
         bank[0] = jnp.zeros(bank.shape[1:], BF)
     X[12] = jnp.zeros(X.shape[1:], BF)
+    for part, lo in ((ref.P_fourth, 9), (ref.P_third, 18)):
+        part[:, :, lo:] = jnp.zeros(part.shape[:2] + (part.shape[2] - lo,) + part.shape[3:], BF)
 
     halo_send, halo_recv = ref.halo_send, ref.halo_recv
 
@@ -118,13 +121,27 @@
         to_down = remote(src_down, dst_down, halo_send.at[index, 1], halo_recv.at[index, 1], down_id)
         return to_up, to_down
 
-    def start_exchange(pair):
-        pl.when(has_up)(lambda: pair[0].start())
-        pl.when(has_down)(lambda: pair[1].start())
-
-    def receive(pair):
-        pl.when(has_down)(lambda: pair[0].wait_recv())
-        pl.when(has_up)(lambda: pair[1].wait_recv())
+    near_up = jnp.logical_and(k == 0, has_up)
+    near_down = jnp.logical_and(k == 1, has_down)
+
+    def pair_at(h):
+        return h + k * (2 - 2 * h)
+
+    def start_near(pair):
+        pl.when(near_up)(lambda: pair[0].start())
+        pl.when(near_down)(lambda: pair[1].start())
+
+    def start_far(pair):
+        pl.when(k == 0)(lambda: pair[1].start())
+        pl.when(k == 1)(lambda: pair[0].start())
+
+    def receive_near(pair):
+        pl.when(near_up)(lambda: pair[1].wait_recv())
+        pl.when(near_down)(lambda: pair[0].wait_recv())
+
+    def receive_far(pair):
+        pl.when(k == 0)(lambda: pair[0].wait_recv())
+        pl.when(k == 1)(lambda: pair[1].wait_recv())
 
     def sent(pair):
         pl.when(has_up)(lambda: pair[0].wait_send())
@@ -152,8 +169,10 @@
 
     peers = (z_n - 1 + canvas_n - 1) if fused else 0
     pl.semaphore_wait(barrier, peers + has_up.astype(jnp.int32) + has_down.astype(jnp.int32))
-    start_exchange(x_halo)
-    start_exchange(co_halo)
+    start_near(x_halo)
+    start_far(x_halo)
+    start_far(co_halo)
+    start_near(co_halo)
 
     def widen(value):
         left = (pltpu.roll(value, 1, 0) * GL[...]).astype(BF)
@@ -269,12 +288,6 @@
                     1 + row_tap, col_tap * part : (col_tap + 1) * part
                 ]
 
-    receive(x_halo)
-    for row in (0, 1, 2, 3, 8, 9, 10, 11):
-        widen_input(row)
-    for h in (-1, 3, -3, 5):
-        first_pair(h)
-
     pooled_buf = ref.POOL
 
     def second_pair(h):
@@ -282,25 +295,18 @@
         acts = []
         for j in (0, 1):
             act, slope = silu_and_slope(both[:, j * ch : (j + 1) * ch] + b_second)
-            if 0 <= h + j < 4:
-                S2[h + j] = slope
+            S2[h + j + 2] = slope
             put_wide(V3J, h + j + 2, act, base=ch, stride=2 * ch)
             rounded = act.astype(BF)
             VJ[h + j + 3, :, ch:] = rounded
             acts.append(rounded.astype(F32))
-        if 0 <= h < 4:
-            SB[...] = acts[0] + acts[1]
-            pooled_buf[h // 2] = (
-                (SB[pl.ds(0, half, stride=2), :] + SB[pl.ds(1, half, stride=2), :]) * 0.25
-            ).astype(BF)
-
-    for h in (0, 2, -2, 4):
-        second_pair(h)
-    out_pool = fetch(pooled_buf, ref.pooled.at[0])
-
-    receive(co_halo)
-    up_rows(0)
-    up_rows(3)
+        return acts
+
+    def pool(acts, place):
+        SB[...] = acts[0] + acts[1]
+        pooled_buf[place] = (
+            (SB[pl.ds(0, half, stride=2), :] + SB[pl.ds(1, half, stride=2), :]) * 0.25
+        ).astype(BF)
 
     def third_pair(h):
         both = conv_pair(V3J, h + 2, KB3, h)
@@ -310,18 +316,39 @@
             put_wide(V3C, h + j + 1, act)
             VC[h + j + 2] = act.astype(BF)
 
-    for h in (1, -1, 3):
-        third_pair(h)
+    receive_far(x_halo)
+    for row in range(4):
+        widen_input(8 - 8 * k + row)
+    first_pair(pair_at(3))
+    first_pair(pair_at(5))
+    pool(second_pair(pair_at(2)), 1 - k)
+    second_pair(pair_at(4))
+    receive_far(co_halo)
+    up_rows(3 - 3 * k)
+    third_pair(pair_at(3))
+
+    receive_near(x_halo)
+    for row in range(4):
+        widen_input(8 * k + row)
+    first_pair(pair_at(-1))
+    first_pair(pair_at(-3))
+    pool(second_pair(pair_at(0)), k)
+    out_pool = fetch(pooled_buf, ref.pooled.at[0])
+    third_pair(1)
+    second_pair(pair_at(-2))
+    receive_near(co_halo)
+    up_rows(3 * k)
+    third_pair(pair_at(-1))
 
     G34, G33, G32, G31 = ref.G34, ref.G33, ref.G32, ref.G31
-    DB = ref.DB
     COT, ACT = ref.COT, ref.ACT
     in_cot.wait()
     in_cp.wait()
     sums = {}
 
-    def add_sum(name, value):
+    def add_sum(name, value, own=None):
         part = jnp.sum(value.reshape(-1, 8, ch), axis=0)
+        part = part if own is None else part * own
         sums[name] = part if name not in sums else sums[name] + part
 
     def fourth_pair(h):
@@ -335,98 +362,124 @@
             add_sum(FOURTH, g)
             put_wide(G34, h + j + 2, g)
 
-    fourth_pair(0)
-    pl.when(has_up)(lambda: g4_halo[0].start())
-    fourth_pair(2)
-    pl.when(has_down)(lambda: g4_halo[1].start())
+    fourth_pair(pair_at(0))
+    start_near(g4_halo)
+    fourth_pair(pair_at(2))
+    start_far(g4_halo)
     out_act = fetch(ACT, ref.activations.at[0])
 
     partner = (c, r + 1 - 2 * k)
 
     class Reduction:
         def __init__(self, index, name):
-            self.index, self.name = index, name
             self.part, self.twin = getattr(ref, "P_" + name), getattr(ref, "RA_" + name)
             self.sums, self.along = getattr(ref, "Q_" + name), getattr(ref, "RB_" + name)
-            self.slots = getattr(ref, "RC_" + name)
-            self.send, self.recv = ref.red_send, ref.red_recv
-
-        def copies_z(self):
+            self.total, self.slots = getattr(ref, "T_" + name), getattr(ref, "RC_" + name)
+            self.index, self.name = index, name
+
+        def copy(self, phase, step, src, dst, device):
+            place = self.index, 4 * phase + step
+            return remote(src, dst, ref.red_send.at[place], ref.red_recv.at[place], device)
+
+        def to_core(self):
+            if fused:
+                self.core = self.copy(0, 0, self.part.at[1 - k], self.twin, partner)
+                self.core.start()
+
+        def join_core(self):
+            self.core.wait_recv()
+            return self.part[k].astype(F32) + self.twin[...].astype(F32)
+
+        def scatter(self, phase, own, n, src, dst, device):
             found = []
-            for step in range(1, z_n):
-                other = lax.rem(z + step, z_n)
-                source = lax.rem(z + z_n - step, z_n)
-                found.append(
-                    remote(
-                        self.sums.at[other], self.along.at[z], self.send.at[self.index, step],
-                        self.recv.at[self.index, step], (c, other * 2 + k),
-                    )
-                )
+            for step in range(1, n):
+                other = lax.rem(own + step, n)
+                found.append(self.copy(phase, step, src.at[other], dst.at[own], device(other)))
+                found[-1].start()
             return found
 
-        def copies_canvas(self):
+        def gather(self, phase, src):
             found = []
             for step in range(1, canvas_n):
                 other = lax.rem(c + step, canvas_n)
-                found.append(
-                    remote(
-                        self.along.at[z], self.slots.at[c], self.send.at[self.index, z_n + step],
-                        self.recv.at[self.index, z_n + step], (other, r),
-                    )
-                )
+                found.append(self.copy(phase, step, src, self.slots.at[c], (other, r)))
+                found[-1].start()
+            self.own = fetch(src, self.slots.at[c])
             return found
 
-        def start_core(self):
-            if not fused:
-                return
-            self.core = remote(
-                self.part.at[1 - k], self.twin, self.send.at[self.index, 0], self.recv.at[self.index, 0], partner
-            )
-            self.core.start()
-
-        def start_z(self):
-            if not fused:
-                return
-            self.core.wait_recv()
-            self.sums[...] = (self.part[k].astype(F32) + self.twin[...].astype(F32)).astype(self.sums.dtype)
-            self.along_copies = self.copies_z()
-            for copy in self.along_copies:
-                copy.start()
-
-        def start_canvas(self):
-            if not fused:
-                return
-            for copy in self.along_copies:
-                copy.wait()
-            self.along[z] = self.sums[z]
-            total = self.along[0].astype(F32)
-            for place in range(1, z_n):
-                total = total + self.along[place].astype(F32)
-            self.along[z] = total.astype(self.along.dtype)
-            self.canvas = self.copies_canvas()
-            for copy in self.canvas:
-                copy.start()
-            self.own = fetch(self.along.at[z], self.slots.at[c])
+        def collect(self, copies, own, n, src, dst):
+            for copy in copies:
+                copy.wait_recv()
+            total = src[own].astype(F32)
+            for step in range(1, n):
+                total = total + dst[lax.rem(own + step, n)].astype(F32)
+            return total
+
+        def to_z(self):
+            if fused:
+                self.sums[...] = self.join_core().astype(BF)
+                self.z_copies = self.scatter(1, z, z_n, self.sums, self.along, lambda other: (c, other * 2 + k))
+
+        def to_canvas(self):
+            if fused:
+                total = self.collect(self.z_copies, z, z_n, self.sums, self.along)
+                self.total[...] = total.astype(BF)
+                self.last = self.gather(2, self.total)
 
         def finish(self):
             if not fused:
                 fetch(self.part, self.slots).wait()
                 return
             self.core.wait_send()
-            for copy in self.canvas:
+            for copy in self.z_copies:
+                copy.wait_send()
+            for copy in self.last:
                 copy.wait()
             self.own.wait()
 
-    red = {name: Reduction(index, name) for index, name in enumerate(LAYERS + (BIAS,))}
+    class WideReduction(Reduction):
+        def to_quarters(self):
+            if fused:
+                total = self.join_core()
+                quarter = total.shape[1] // canvas_n
+                for place in range(canvas_n):
+                    self.sums[place] = total[:, place * quarter : (place + 1) * quarter].astype(BF)
+                self.c_copies = self.scatter(1, c, canvas_n, self.sums, self.along, lambda other: (other, r))
+
+        def to_z(self):
+            if fused:
+                total = self.collect(self.c_copies, c, canvas_n, self.sums, self.along)
+                self.zs, self.zl = getattr(ref, "ZS_" + self.name), getattr(ref, "ZL_" + self.name)
+                self.zs[...] = total.astype(BF)
+                self.z_copies = self.scatter(2, z, z_n, self.zs, self.zl, lambda other: (c, other * 2 + k))
+
+        def to_canvas(self):
+            if fused:
+                total = self.collect(self.z_copies, z, z_n, self.zs, self.zl)
+                self.total[...] = total.astype(BF)
+                self.last = self.gather(3, self.total)
+
+        def finish(self):
+            if fused:
+                for copy in self.c_copies:
+                    copy.wait_send()
+            super().finish()
+
+    red = {
+        name: (WideReduction if name in WIDE else Reduction)(index, name) for index, name in enumerate(LAYERS)
+    }
 
     def put_parts(name, value):
         part = getattr(ref, "P_" + name)
-        blocks, share = part.shape[2], part.shape[3]
+        blocks, lanes = value.shape[0] // ch, value.shape[1] // 128
         for block in range(blocks):
-            place = block if name == UP else blocks - 1 - block
+            first = (block if name == UP else blocks - 1 - block) * lanes
             for owner in range(8):
-                lo = block * ch + owner * share
-                part[owner % 2, owner // 2, place] = value[lo : lo + share].astype(BF)
+                lo = block * ch + owner * 16
+                for lane in range(lanes):
+                    part[owner % 2, owner // 2, first + lane] = value[
+                        lo : lo + 16, lane * 128 : (lane + 1) * 128
+                    ].astype(BF)
 
     def row_stack(src, off, h):
         return jnp.concatenate(
@@ -439,81 +492,89 @@
         return dot_tn(band, stacked)
 
     def load_wide(dst, row, src):
-        put_wide(dst, row, src.astype(F32))
+        put_wide(dst, row, src[row].astype(F32))
+
+    def is_own(row):
+        return jnp.logical_and(row >= 0, row < 4).astype(F32)
 
     def third_back(h):
         both = back_pair(G34, h + 2, KT4, h)
         for j in (0, 1):
             g = (both[:, j * ch : (j + 1) * ch] * S3[h + j + 1]).astype(BF).astype(F32)
-            if 0 <= h + j < 4:
-                add_sum(THIRD, g)
+            add_sum(THIRD, g, is_own(h + j))
             put_wide(G33, h + j + 1, g)
 
     put_parts(FOURTH, weight_grad(G34, 2, VC, 2))
-    red[FOURTH].start_core()
+    red[FOURTH].to_core()
     third_back(1)
-    receive(g4_halo)
-    for row in (0, 1, 6, 7):
-        load_wide(G34, row, G4[row])
-    third_back(-1)
-    third_back(3)
-    red[FOURTH].start_z()
+    receive_far(g4_halo)
+    for row in (0, 1):
+        load_wide(G34, 6 - 6 * k + row, G4)
+    third_back(pair_at(3))
+    if fused:
+        red[FOURTH].to_quarters()
+    receive_near(g4_halo)
+    for row in (0, 1):
+        load_wide(G34, 6 * k + row, G4)
+    third_back(pair_at(-1))
 
     GB, CP = ref.GB, ref.CP
 
     def joined_back(h):
-        band = jnp.concatenate([G33[h + 1 + d] for d in (-1, 0, 1)], axis=1)
-        weights = jnp.concatenate([KT3[link(h)], KT3[2], KT3[link(h + 1) * 3]], axis=1)
-        d_joined = dot_nt(band, weights)
-        g_up = d_joined[:, :ch].astype(BF).astype(F32)
-        add_sum(UP, g_up)
-        a = h % 2
-        SA[a] = g_up
-        for b in (0, 1):
-            lo = (2 * a + b) * ch
-            GB[h // 2, :, lo : lo + ch] = SA[a, pl.ds(b, half, stride=2), :].astype(BF)
-        if a == 0:
-            spread = CP[h // 2].astype(F32) * 0.25
-            SB[pl.ds(0, half, stride=2), :] = spread
-            SB[pl.ds(1, half, stride=2), :] = spread
-        g = ((d_joined[:, ch:] + SB[...]) * S2[h]).astype(BF)
-        G2[h + 2] = g
-        g = g.astype(F32)
-        add_sum(SECOND, g)
-        put_wide(G32, h + 2, g)
-
-    joined_back(0)
-    joined_back(1)
-    pl.when(has_up)(lambda: g2_halo[0].start())
-    joined_back(2)
-    joined_back(3)
-    pl.when(has_down)(lambda: g2_halo[1].start())
-
+        i = h // 2
+        spread = CP[i].astype(F32) * 0.25
+        SB[pl.ds(0, half, stride=2), :] = spread
+        SB[pl.ds(1, half, stride=2), :] = spread
+        for a in (0, 1):
+            row = h + a
+            band = jnp.concatenate([G33[row + 1 + d] for d in (-1, 0, 1)], axis=1)
+            weights = jnp.concatenate([KT3[link(row)], KT3[2], KT3[link(row + 1) * 3]], axis=1)
+            d_joined = dot_nt(band, weights)
+            g_up = d_joined[:, :ch].astype(BF).astype(F32)
+            add_sum(UP, g_up)
+            SA[a] = g_up
+            for b in (0, 1):
+                lo = (2 * a + b) * ch
+                GB[i, :, lo : lo + ch] = SA[a, pl.ds(b, half, stride=2), :].astype(BF)
+            g = ((d_joined[:, ch:] + SB[...]) * S2[row + 2]).astype(BF)
+            G2[row + 2] = g
+            g = g.astype(F32)
+            add_sum(SECOND, g)
+            put_wide(G32, row + 2, g)
+
+    joined_back(pair_at(0))
+    start_near(g2_halo)
     put_parts(THIRD, weight_grad(G33, 1, VJ, 3))
-    red[THIRD].start_core()
-    red[FOURTH].start_canvas()
+    red[THIRD].to_core()
+    red[FOURTH].to_z()
+    joined_back(pair_at(2))
+    start_far(g2_halo)
+    if fused:
+        red[THIRD].to_quarters()
+    put_parts(SECOND, weight_grad(G32, 2, VA, 4))
+    red[SECOND].to_core()
     bands = GB[...].reshape(2 * half, 4 * ch)
     put_parts(UP, dot_tn(bands, CO[1:3].reshape(2 * half, c_coarse)))
-    red[UP].start_core()
-    red[THIRD].start_z()
-    put_parts(SECOND, weight_grad(G32, 2, VA, 4))
-    red[SECOND].start_core()
-    red[UP].start_z()
+    red[UP].to_core()
 
     def first_back(h):
         both = back_pair(G32, h + 2, KT2, h)
         for j in (0, 1):
             g = (both[:, j * ch : (j + 1) * ch] * S1[h + j + 3]).astype(BF).astype(F32)
-            if 0 <= h + j < 4:
-                add_sum(FIRST, g)
+            add_sum(FIRST, g, is_own(h + j))
             put_wide(G31, h + j + 1, g)
 
     first_back(1)
-    receive(g2_halo)
-    for row in (0, 1, 6, 7):
-        load_wide(G32, row, G2[row])
-    first_back(-1)
-    first_back(3)
+    receive_far(g2_halo)
+    for row in (0, 1):
+        load_wide(G32, 6 - 6 * k + row, G2)
+    first_back(pair_at(3))
+    red[FOURTH].to_canvas()
+    red[SECOND].to_z()
+    receive_near(g2_halo)
+    for row in (0, 1):
+        load_wide(G32, 6 * k + row, G2)
+    first_back(pair_at(-1))
 
     def pick(h, joined):
         return X[12 + joined * (h - 8)]
@@ -525,17 +586,17 @@
         ],
         axis=1,
     )
-    put_parts(FIRST, dot_nn(stacked, G31[1:5].reshape(4 * width, 3 * ch)).T)
-    red[FIRST].start_core()
+    grad = dot_nn(stacked, G31[1:5].reshape(4 * width, 3 * ch)).T
+    put_parts(FIRST, jnp.concatenate([grad, jnp.zeros((3 * ch, 256 - 3 * c_in), F32)], axis=1))
+    DB = ref.DB
+    DB[...] = jnp.zeros(DB.shape, F32)
     for place, name in enumerate(ORDER):
         DB[place : place + 1] = jnp.sum(sums[name], axis=0, keepdims=True)
-    if fused:
-        ref.P_bias[0] = DB[...]
-        ref.P_bias[1] = DB[...]
-    else:
-        ref.P_bias[0] = DB[...]
-    red[BIAS].start_core()
-    red[SECOND].start_z()
+    for owner in range(8):
+        ref.P_first[owner % 2, owner // 2, 6] = DB[...].astype(BF)
+    red[FIRST].to_core()
+    red[UP].to_z()
+    red[THIRD].to_z()
 
     GI = ref.GI
 
@@ -546,7 +607,7 @@
         GI[h] = both[:c_in]
         GI[h + 1] = both[c_in:]
 
-    red[FIRST].start_z()
+    red[FIRST].to_z()
     input_back(0)
     input_back(2)
     out_gi = fetch(GI, ref.grad_inputs.at[0])
@@ -554,29 +615,12 @@
     for i in (0, 1):
         GC[i] = dot_nt(GB[i], WU[...]).astype(BF)
     out_gc = fetch(GC, ref.grad_coarse.at[0])
-    red[THIRD].start_canvas()
-    red[UP].start_canvas()
-    red[SECOND].start_canvas()
-
-    if fused:
-        bias_red = red[BIAS]
-        bias_red.core.wait_recv()
-        bias_red.sums[z] = bias_red.part[k] + bias_red.twin[...]
-        bias_red.along_copies = []
-        for step in range(1, z_n):
-            other = lax.rem(z + step, z_n)
-            bias_red.along_copies.append(
-                remote(
-                    bias_red.sums.at[z], bias_red.along.at[z], bias_red.send.at[bias_red.index, step],
-                    bias_red.recv.at[bias_red.index, step], (c, other * 2 + k),
-                )
-            )
-        for copy in bias_red.along_copies:
-            copy.start()
-    red[FIRST].start_canvas()
-    red[BIAS].start_canvas()
-
-    for name in LAYERS + (BIAS,):
+    red[SECOND].to_canvas()
+    red[UP].to_canvas()
+    red[THIRD].to_canvas()
+    red[FIRST].to_canvas()
+
+    for name in LAYERS:
         red[name].finish()
     for pair in (x_halo, co_halo, g4_halo, g2_halo):
         sent(pair)
@@ -584,43 +628,69 @@
         copy.wait()
 
 
-def finish_kernel(names, sizes, *refs):
+def finish_kernel(names, staged, sizes, *refs):
     ref = types.SimpleNamespace(**dict(zip(names, refs)))
-    ref.held, ref.sem = refs[-5:-1], refs[-1]
+    held = types.SimpleNamespace(**dict(zip(staged, refs[len(names) : -1])))
+    sem = refs[-1]
     ch, share = sizes
     r = lax.axis_index("rows")
-    copies = []
-    for place, name in enumerate(BIG):
-        held = ref.held[place]
-        enter = pltpu.make_async_copy(getattr(ref, name), held, ref.sem.at[0, place])
-        leave = pltpu.make_async_copy(held, getattr(ref, "out_" + name), ref.sem.at[1, place])
-        enter.start()
-        copies.append((enter, leave))
-
-    def total(slots):
-        value = slots[0].astype(F32)
-        for place in range(1, slots.shape[0]):
-            value = value + slots[place].astype(F32)
-        return value
-
-    for name in (FIRST, SECOND, THIRD, FOURTH):
-        value = total(getattr(ref, "RC_" + name))
-        out = getattr(ref, "out_w_" + name)
-        part = out.shape[3]
-        for row_tap in range(3):
-            out[row_tap] = value[:, :, row_tap * part : (row_tap + 1) * part]
-    value = total(ref.RC_up)
-    for a in (0, 1):
-        for b in (0, 1):
-            ref.out_w_up[a, b] = value[2 * a + b]
-    sums = pltpu.roll(total(ref.RC_bias), lax.rem(ch - r * share, ch), 1)
-    for place, name in enumerate(ORDER):
-        getattr(ref, "out_b_" + name)[...] = sums[place : place + 1, :share]
-    for enter, leave in copies:
-        enter.wait()
-        leave.start()
-    for enter, leave in copies:
-        leave.wait()
+    enter, leave = {}, {}
+    for place, name in enumerate(staged):
+        stage = getattr(held, name)
+        if name in BIG or name.startswith("RC"):
+            enter[name] = pltpu.make_async_copy(getattr(ref, name), stage, sem.at[0, place])
+            enter[name].start()
+        if name in BIG or name.startswith("w"):
+            leave[name] = pltpu.make_async_copy(stage, getattr(ref, "out_" + name), sem.at[1, place])
+
+    def tiles(name):
+        slots = getattr(held, "RC_" + name)
+        if name in WIDE:
+            quarter = slots.shape[1]
+            return lambda t: slots[t // quarter, t % quarter].astype(F32)
+
+        def total(t):
+            value = slots[0, t].astype(F32)
+            for place in range(1, slots.shape[0]):
+                value = value + slots[place, t].astype(F32)
+            return value
+
+        return total
+
+    for name in BIG + LAYERS:
+        if name in BIG:
+            enter[name].wait()
+            leave[name].start()
+            continue
+        enter["RC_" + name].wait()
+        tile = tiles(name)
+        out = getattr(held, "w_" + name)
+        if name == FIRST:
+            part = out.shape[3]
+            for col_tap in range(3):
+                for row_tap in range(3):
+                    value = tile(2 * col_tap + row_tap // 2)
+                    lo = part * (row_tap % 2)
+                    out[row_tap, col_tap] = value[:, lo : lo + part]
+            sums = pltpu.roll(tile(6), lax.rem(ch - r * share, ch), 1)
+            for place, layer in enumerate(ORDER):
+                getattr(ref, "out_b_" + layer)[...] = sums[place : place + 1, :share]
+        elif name == UP:
+            for a in (0, 1):
+                for b in (0, 1):
+                    for lane in (0, 1):
+                        out[a, b, :, lane * 128 : (lane + 1) * 128] = tile(4 * a + 2 * b + lane)
+        else:
+            lanes = out.shape[3] // 128
+            for col_tap in range(3):
+                for row_tap in range(3):
+                    for lane in range(lanes):
+                        out[row_tap, col_tap, :, lane * 128 : (lane + 1) * 128] = tile(
+                            (3 * col_tap + row_tap) * lanes + lane
+                        )
+        leave["w_" + name].start()
+    for copy in leave.values():
+        copy.wait()
 
 
 def on_device(
@@ -689,14 +759,7 @@
 
     owners, z_n = 8, 4
     share = ch // owners
-    pieces = dict(
-        fourth=((3, share, 3 * ch), BF),
-        third=((3, share, 6 * ch), BF),
-        up=((4, share, c_coarse), BF),
-        second=((3, share, 3 * ch), BF),
-        first=((3, share, 3 * c_in), BF),
-        bias=((8, ch), F32),
-    )
+    tiles = dict(fourth=12, third=20, up=8, second=9, first=7)
     outs = dict(
         activations=jax.ShapeDtypeStruct((1, 4, width, ch), BF),
         pooled=jax.ShapeDtypeStruct((1, 2, half, ch), BF),
@@ -727,7 +790,7 @@
         VJ=pltpu.VMEM((9, width, 2 * ch), BF),
         VC=pltpu.VMEM((7, width, ch), BF),
         S1=pltpu.VMEM((10, width, ch), F32),
-        S2=pltpu.VMEM((4, width, ch), F32),
+        S2=pltpu.VMEM((8, width, ch), F32),
         S3=pltpu.VMEM((6, width, ch), F32),
         G4=pltpu.VMEM((8, width, ch), BF),
         G2=pltpu.VMEM((8, width, ch), BF),
@@ -738,7 +801,7 @@
         GB=pltpu.VMEM((2, half, 4 * ch), BF),
         SA=pltpu.VMEM((2, width, ch), F32),
         SB=pltpu.VMEM((width, ch), F32),
-        DB=pltpu.VMEM((8, ch), F32),
+        DB=pltpu.VMEM((16, ch), F32),
         ACT=pltpu.VMEM((4, width, ch), BF),
         POOL=pltpu.VMEM((2, half, ch), BF),
         GI=pltpu.VMEM((4, c_in, width), BF),
@@ -746,23 +809,32 @@
         local_sem=pltpu.SemaphoreType.DMA((24,)),
         halo_send=pltpu.SemaphoreType.DMA((4, 2)),
         halo_recv=pltpu.SemaphoreType.DMA((4, 2)),
-        red_send=pltpu.SemaphoreType.DMA((6, z_n + canvas_n)),
-        red_recv=pltpu.SemaphoreType.DMA((6, z_n + canvas_n)),
+        red_send=pltpu.SemaphoreType.DMA((5, 16)),
+        red_recv=pltpu.SemaphoreType.DMA((5, 16)),
     )
-    for name, (shape, kind) in pieces.items():
-        if name == BIAS:
-            scratch["P_bias"] = pltpu.VMEM((2,) + shape, kind)
-            scratch["RA_bias"] = pltpu.VMEM(shape, kind)
+    for name, count in tiles.items():
+
+        def buffer(*lead):
+            return pltpu.VMEM(lead + (16, 128), BF)
+
+        landing = (canvas_n, count, 16, 128)
+        scratch["P_" + name] = buffer(2, z_n, count)
+        scratch["RA_" + name] = buffer(z_n, count)
+        if name in WIDE:
+            quarter = count // 4
+            scratch["Q_" + name] = buffer(4, z_n, quarter)
+            scratch["RB_" + name] = buffer(4, z_n, quarter)
+            scratch["ZS_" + name] = buffer(z_n, quarter)
+            scratch["ZL_" + name] = buffer(z_n, quarter)
+            scratch["T_" + name] = buffer(quarter)
+            landing = (4, quarter, 16, 128)
         else:
-            scratch["P_" + name] = pltpu.VMEM((2, z_n) + shape, kind)
-            scratch["RA_" + name] = pltpu.VMEM((z_n,) + shape, kind)
-        scratch["Q_" + name] = pltpu.VMEM((z_n,) + shape, kind)
-        scratch["RB_" + name] = pltpu.VMEM((z_n,) + shape, kind)
-        if fused:
-            landing = (canvas_n,) + shape
-        else:
-            landing = scratch["P_" + name].shape
-        outs["RC_" + name] = jax.ShapeDtypeStruct(landing, kind)
+            scratch["Q_" + name] = buffer(z_n, count)
+            scratch["RB_" + name] = buffer(z_n, count)
+            scratch["T_" + name] = buffer(count)
+        if not fused:
+            landing = (2, z_n, count, 16, 128)
+        outs["RC_" + name] = jax.ShapeDtypeStruct(landing, BF)
 
     names = list(arg) + list(outs) + list(scratch)
     sizes = (width, ch, c_in, c_coarse, rows_n, canvas_n, fused)
@@ -783,18 +855,24 @@
         return unfused_tail(held, rows_n, ch, c_in, c_coarse)
 
     done = {"out_" + name: outs[name] for name in BIG}
-    for name in (FIRST, SECOND, THIRD, FOURTH):
-        shape = pieces[name][0]
-        done["out_w_" + name] = jax.ShapeDtypeStruct((3, 3, share, shape[2] // 3), F32)
-    done["out_w_up"] = jax.ShapeDtypeStruct((2, 2, share, c_coarse), F32)
-    for name in ORDER:
+    parts = dict(first=c_in, second=ch, third=2 * ch, fourth=ch)
+    for name in LAYERS:
+        if name == UP:
+            shape = (2, 2, share, c_coarse)
+        else:
+            shape = (3, 3, share, parts[name])
+        done["out_w_" + name] = jax.ShapeDtypeStruct(shape, F32)
+    for name in LAYERS:
         done["out_b_" + name] = jax.ShapeDtypeStruct((1, share), F32)
+    staged = {name: outs[name] for name in outs}
+    staged.update({"w_" + name: done["out_w_" + name] for name in LAYERS})
     finals = pl.pallas_call(
-        functools.partial(finish_kernel, list(outs) + list(done), (ch, share)),
+        functools.partial(finish_kernel, list(outs) + list(done), list(staged), (ch, share)),
         out_shape=tuple(done.values()),
-        in_specs=[any_spec if name in BIG else vmem_spec for name in outs],
-        out_specs=tuple(any_spec if name[4:] in BIG else vmem_spec for name in done),
-        scratch_shapes=[pltpu.VMEM(outs[name].shape, BF) for name in BIG] + [pltpu.SemaphoreType.DMA((2, 4))],
+        in_specs=[any_spec] * len(outs),
+        out_specs=tuple(vmem_spec if name.startswith("out_b") else any_spec for name in done),
+        scratch_shapes=[pltpu.VMEM(like.shape, like.dtype) for like in staged.values()]
+        + [pltpu.SemaphoreType.DMA((2, len(staged)))],
         name="finish",
     )(*results)
     final = dict(zip(done, finals))
@@ -825,18 +903,25 @@
 
     def whole(name):
         parts = held["RC_" + name].astype(F32)
-        blocks, piece, lanes = parts.shape[2:]
-        parts = jnp.transpose(parts, (2, 1, 0, 3, 4)).reshape(blocks, ch, lanes)
+        return jnp.transpose(parts, (2, 1, 0, 3, 4)).reshape(-1, ch, 128)
+
+    tiles = lax.psum({name: whole(name) for name in LAYERS}, ("canvas", "rows"))
+    weights = {}
+    for name in LAYERS:
         if name == UP:
-            return parts.reshape(2, 2, ch, lanes)
-        return jnp.transpose(parts.reshape(3, ch, 3, lanes // 3), (2, 0, 1, 3))
-
-    weights = {name: whole(name) for name in LAYERS}
-    weights, biases = lax.psum((weights, held["RC_bias"][0]), ("canvas", "rows"))
-    weights = {name: lax.dynamic_slice_in_dim(value, offset, share, 2) for name, value in weights.items()}
-    biases = lax.dynamic_slice_in_dim(biases, offset, share, 1)
-    places = {FIRST: 0, SECOND: 1, UP: 2, THIRD: 3, FOURTH: 4}
-    return ordered(held, weights, {name: biases[place] for name, place in places.items()})
+            value = tiles[name].reshape(4, 1, 2, ch, 128)
+        elif name == FIRST:
+            value = jnp.swapaxes(tiles[name][:6].reshape(3, 2, ch, 128), 1, 2).reshape(3, ch, 256)
+            value = jnp.transpose(value[..., : 3 * c_in].reshape(3, ch, 3, c_in), (0, 2, 1, 3))[:, :, None]
+        else:
+            lanes = 2 if name == THIRD else 1
+            value = tiles[name][: 9 * lanes].reshape(3, 3, lanes, ch, 128)
+        value = jnp.transpose(value, (1, 0, 3, 2, 4)).reshape(value.shape[1], value.shape[0], ch, -1)
+        if name == UP:
+            value = value.reshape(2, 2, ch, c_coarse)
+        weights[name] = lax.dynamic_slice_in_dim(value, offset, share, 2)
+    biases = lax.dynamic_slice_in_dim(tiles[FIRST][6], offset, share, 1)
+    return ordered(held, weights, {name: biases[place] for place, name in enumerate(ORDER)})
 
 
 def solution(mesh):

time: 58.2 us -> 52.1 us (0.90)
  Pallas kernels: 57.2 us -> 51.1 us
    pallas_call x1, Pallas kernels: 53.3 us -> 48.3 us  [on_device(): pl.pallas_call(functools.partial(level_kernel, names, sizes), out_shape=t...]
    pallas_call x1, Pallas kernels: 3.93 us -> 2.84 us  [on_device(): pl.pallas_call(functools.partial(finish_kernel, list(outs) + list(done),...]
where the time goes in v2:
time: 52.1 us; the launch traced here: 51.9 us
  Pallas kernels  51.1 us (98%)
  between operations  0.82 us (2%)
    pallas_call x1, Pallas kernels, on_device(): pl.pallas_call(functools.partial(level_kernel, names, sizes), out_shape=t...  48.3 us
    pallas_call x1, Pallas kernels, on_device(): pl.pallas_call(functools.partial(finish_kernel, list(outs) + list(done),...  2.84 us

profile of v2, /device:TPU:0, one launch (start us, length us, event | category | flops | bytes accessed | tf_op | source)
XLA Modules:
  0.0 51.9 jit_solution(9596896174358513417)
XLA Ops:
  0.7 48.3 %level.1 = (bf16[1,4,384,128]{3,2,1,0:T(8,128)(2,1)}, bf16[1,2,192,128]{3,2,1,0:T(8,128)(2,1)}, bf16[1,4,64,384]{3,2,1,0:T(8,128)(2,1)}, bf16[1,2,192,256]{3,2,1...) custom-call(bf16[1,4,64,384]{3,2,1,0:T(8,128)(2,1)} %bitcast.24, ...), custom_call_target="tpu_custom_call" | custom-call | tf_op jit(solution)/shard_map/level/pallas_call | solution.py:841
  48.9 2.8 %finish.1 = (bf16[1,4,384,128]{3,2,1,0:T(8,128)(2,1)}, bf16[1,2,192,128]{3,2,1,0:T(8,128)(2,1)}, bf16[1,4,64,384]{3,2,1,0:T(8,128)(2,1)}, bf16[1,2,192,256]{3,2,...) custom-call(bf16[1,4,384,128]{3,2,1,0:T(8,128)(2,1)} %get-tuple-elem, ...), custom_call_target="tpu_custom_call" | custom-call | tf_op jit(solution)/shard_map/finish/pallas_call | solution.py:869

commit v3 on v2

v3 whole, which is shorter than its diff:
```python
import functools
import types

import jax
import jax.numpy as jnp
from jax import lax
from jax.experimental import pallas as pl
from jax.experimental.pallas import tpu as pltpu
from jax.sharding import PartitionSpec as P

MESH = pl.DeviceIdType.MESH
BF = jnp.bfloat16
F32 = jnp.float32
VMEM_BYTES = 58 * 2**20

FIRST, SECOND, UP, THIRD, FOURTH = "first", "second", "up", "third", "fourth"
THIRD_A, THIRD_B = "third_a", "third_b"
GROUPS = (FOURTH, THIRD_A, THIRD_B, SECOND, UP, FIRST)
WIDE = (FOURTH, THIRD_A, SECOND, UP)
ORDER = (FIRST, SECOND, UP, THIRD, FOURTH)
BIG = ("activations", "pooled", "grad_inputs", "grad_coarse")


def dot_nn(a, b):
    return lax.dot_general(a, b, (((1,), (0,)), ((), ())), preferred_element_type=F32)


def dot_tn(a, b):
    return lax.dot_general(a, b, (((0,), (0,)), ((), ())), preferred_element_type=F32)


def dot_nt(a, b):
    return lax.dot_general(a, b, (((1,), (1,)), ((), ())), preferred_element_type=F32)


def silu_and_slope(values):
    sigma = 0.5 * jnp.tanh(0.5 * values) + 0.5
    act = values * sigma
    return act, sigma + act * (1.0 - sigma)


def level_kernel(names, sizes, *refs):
    ref = types.SimpleNamespace(**dict(zip(names, refs)))
    width, ch, c_in, c_coarse, rows_n, canvas_n, fused = sizes
    half = width // 2
    c = lax.axis_index("canvas")
    r = lax.axis_index("rows")
    z, k = r // 2, lax.rem(r, 2)
    z_n = rows_n // 2

    near_id, far_id = (c, r - 1 + 2 * k), (c, r + 1 - 2 * k)
    has_near = jnp.logical_and(near_id[1] >= 0, near_id[1] < rows_n)

    def flip(index, last):
        return index + k * (last - 2 * index)

    barrier = pltpu.get_barrier_semaphore()

    def greet(device):
        pl.semaphore_signal(barrier, inc=1, device_id=device, device_id_type=MESH)

    pl.when(has_near)(lambda: greet(near_id))
    greet(far_id)
    if fused:
        for step in range(1, z_n):
            greet((c, lax.rem(z + step, z_n) * 2 + k))
        for step in range(1, canvas_n):
            greet((lax.rem(c + step, canvas_n), r))

    used = [0]

    def fetch(src, dst):
        copy = pltpu.make_async_copy(src, dst, ref.local_sem.at[used[0]])
        used[0] += 1
        assert used[0] <= ref.local_sem.shape[0]
        copy.start()
        return copy

    def fetch_taps(weights, bank):
        return [fetch(weights.at[flip(tap, 2)], bank.at[1 + tap]) for tap in range(3)]

    def wait(copies):
        for copy in copies:
            copy.wait()

    X, CO, WU = ref.X, ref.CO, ref.WU
    KB1, KB2, KU3, KB3, KB4 = ref.KB1, ref.KB2, ref.KU3, ref.KB3, ref.KB4
    KT1, KT2, KT3, KT4 = ref.KT1, ref.KT2, ref.KT3, ref.KT4
    in_x = [fetch(ref.inputs.at[0, flip(row, 3)], X.at[4 + row]) for row in range(4)]
    in_w1 = fetch_taps(ref.w_first, KB1)

    def remote(src, dst, send, recv, device):
        return pltpu.make_async_remote_copy(
            src_ref=src, dst_ref=dst, send_sem=send, recv_sem=recv, device_id=device, device_id_type=MESH
        )

    halo_count = [0]

    def exchange(src_near, dst_near, src_far, dst_far):
        place = halo_count[0]
        halo_count[0] += 1
        near = remote(src_near, dst_near, ref.halo_send.at[place, 0], ref.halo_recv.at[place, 0], near_id)
        far = remote(src_far, dst_far, ref.halo_send.at[place, 1], ref.halo_recv.at[place, 1], far_id)
        return near, far

    def start_near(pairs):
        def start():
            for pair in pairs:
                pair[0].start()

        pl.when(has_near)(start)

    def start_far(pairs):
        for pair in pairs:
            pair[1].start()

    def receive_near(pairs):
        def receive():
            for pair in pairs:
                pair[0].wait_recv()

        pl.when(has_near)(receive)

    def receive_far(pairs):
        for pair in pairs:
            pair[1].wait_recv()

    def sent(pairs):
        def near():
            for pair in pairs:
                pair[0].wait_send()

        pl.when(has_near)(near)
        for pair in pairs:
            pair[1].wait_send()

    G4, G2 = ref.G4, ref.G2

    def row_exchange(buffer, row):
        return exchange(
            buffer.at[2 + row], buffer.at[1 - row], buffer.at[5 - row], buffer.at[6 + row]
        )

    x_halo = []
    for row in range(4):
        mine, last = ref.inputs.at[0, flip(row, 3)], ref.inputs.at[0, flip(3 - row, 3)]
        x_halo.append(exchange(mine, X.at[3 - row], last, X.at[8 + row]))
    co_halo = [exchange(ref.coarse.at[0, flip(0, 1)], CO.at[0], ref.coarse.at[0, flip(1, 1)], CO.at[3])]
    g4_halo = [row_exchange(G4, 0), row_exchange(G4, 1)]
    g2_halo, g2_second = [row_exchange(G2, 0)], [row_exchange(G2, 1)]

    in_co = [fetch(ref.coarse.at[0, flip(i, 1)], CO.at[1 + i]) for i in (0, 1)]
    in_up = [
        fetch(ref.w_up.at[flip(a, 1), b], WU.at[:, pl.ds((2 * a + b) * ch, ch)]) for a in (0, 1) for b in (0, 1)
    ]
    in_w2 = fetch_taps(ref.w_second, KB2)
    in_w3 = [
        fetch(ref.w_third.at[flip(tap, 2), :, pl.ds(lo, ch)], bank.at[1 + tap])
        for bank, lo in ((KU3, 0), (KB3, ch))
        for tap in range(3)
    ]
    in_w4 = fetch_taps(ref.w_fourth, KB4)
    in_cot = [fetch(ref.cot_out.at[0, flip(row, 3)], ref.COT.at[row]) for row in range(4)]
    in_cp = [fetch(ref.cot_pool.at[0, flip(i, 1)], ref.CP.at[i]) for i in (0, 1)]

    @pl.when(jnp.logical_not(has_near))
    def _():
        X[0:4] = jnp.zeros((4,) + X.shape[1:], BF)
        CO[0] = jnp.zeros(CO.shape[1:], BF)
        G4[0:2] = jnp.zeros((2,) + G4.shape[1:], BF)
        G2[0:2] = jnp.zeros((2,) + G2.shape[1:], BF)

    first, total_rows = r * 4, rows_n * 4

    def link(h):
        row = first + flip(h, 4)
        inside = jnp.logical_and(row > 0, row < total_rows)
        cut = ref.row_cuts[0, jnp.clip(row, 0, total_rows - 1)]
        return jnp.where(inside, 1 - cut, 0)

    open_row = 1.0 - ref.col_cuts[...].astype(F32)
    open_row = jnp.where(lax.broadcasted_iota(jnp.int32, (1, width), 1) > 0, open_row, 0.0)
    left_gate = jnp.broadcast_to(open_row, (128, width))
    right_gate = pltpu.roll(left_gate, width - 1, 1)
    GL, GR = ref.GL, ref.GR
    GL[...] = left_gate.T
    GR[...] = right_gate.T
    left_row, right_row = left_gate[:c_in], right_gate[:c_in]

    for bank in (KB1, KB2, KU3, KB3, KB4, KT1, KT2, KT3, KT4, ref.VA, ref.VJ, ref.VC):
        bank[0] = jnp.zeros(bank.shape[1:], BF)
    X[12] = jnp.zeros(X.shape[1:], BF)
    for part in (ref.P_fourth, ref.P_third_a, ref.P_third_b, ref.P_second):
        if part.shape[2] > 9:
            part[:, :, 9:] = jnp.zeros(part.shape[:2] + (part.shape[2] - 9,) + part.shape[3:], BF)

    peers = (z_n - 1 + canvas_n - 1) if fused else 0
    pl.semaphore_wait(barrier, peers + 1 + has_near.astype(jnp.int32))
    start_near(x_halo)
    start_far(x_halo)
    start_far(co_halo)

    def put_wide(dst, row, value, base=0, stride=ch):
        left = (pltpu.roll(value, 1, 0) * GL[...]).astype(BF)
        right = (pltpu.roll(value, width - 1, 0) * GR[...]).astype(BF)
        for place, piece in enumerate((left, value.astype(BF), right)):
            lo = base + place * stride
            dst[row, :, lo : lo + ch] = piece

    def taps(bank, h):
        ga, gb, gc = link(h), link(h + 1), link(h + 2)
        found = bank[0], bank[ga], bank[2], bank[gb * 3], bank[gb], bank[gc * 3]
        return [tap.reshape(-1, tap.shape[-1]) for tap in found]

    def forward_weights(bank, h):
        zero, up0, mid, down0, up1, down1 = taps(bank, h)
        return jnp.concatenate(
            [
                jnp.concatenate([up0, mid, down0, zero], axis=0),
                jnp.concatenate([zero, up1, mid, down1], axis=0),
            ],
            axis=1,
        )

    def back_weights(bank, h):
        zero, up0, mid, down0, up1, down1 = taps(bank, h)
        return jnp.concatenate(
            [
                jnp.concatenate([up0, mid, down0, zero], axis=1),
                jnp.concatenate([zero, up1, mid, down1], axis=1),
            ],
            axis=0,
        )

    def band(src, at, reach=(-1, 0, 1, 2)):
        return jnp.concatenate([src[at + d] for d in reach], axis=1)

    def conv_pair(src, at, bank, h):
        return dot_nn(band(src, at), forward_weights(bank, h))

    def back_pair(src, at, bank, h):
        return dot_nt(band(src, at), back_weights(bank, h))

    def back_row(src, at, bank, h):
        weights = jnp.concatenate([bank[link(h)], bank[2], bank[link(h + 1) * 3]], axis=1)
        return dot_nt(band(src, at, (-1, 0, 1)), weights)

    def bias(layer):
        return getattr(ref, "b_" + layer)[...].astype(F32).reshape(1, ch)

    b_first, b_second, b_up, b_third, b_fourth = (bias(layer) for layer in ORDER)
    V3X, V3A, V3U, V3B, V3C = ref.V3X, ref.V3A, ref.V3U, ref.V3B, ref.V3C
    VA, VJ, VC = ref.VA, ref.VJ, ref.VC
    S1, S2, S3 = ref.S1, ref.S2, ref.S3
    SA, SB = ref.SA, ref.SB

    def widen_input(row):
        value = X[row].astype(F32)
        V3X[row, 0:c_in] = (pltpu.roll(value, 1, 1) * left_row).astype(BF)
        V3X[row, c_in : 2 * c_in] = X[row]
        V3X[row, 2 * c_in : 3 * c_in] = (pltpu.roll(value, width - 1, 1) * right_row).astype(BF)

    def first_pair(h):
        rows = V3X[h + 3 : h + 7].reshape(4 * 3 * c_in, width)
        both = dot_tn(rows, forward_weights(KB1, h))
        for j in (0, 1):
            act, slope = silu_and_slope(both[:, j * ch : (j + 1) * ch] + b_first)
            if -1 <= h + j < 5:
                S1[h + j + 1] = slope
                VA[h + j + 2] = act.astype(BF)
            put_wide(V3A, h + j + 3, act)

    def up_rows(i):
        fine = dot_nn(CO[i], WU[...])
        for a in (0, 1):
            for b in (0, 1):
                lo = (2 * a + b) * ch
                SA[a, pl.ds(b, half, stride=2), :] = (fine[:, lo : lo + ch] + b_up).astype(BF).astype(F32)
        for a in (0, 1):
            value = SA[a]
            row = 2 * i + a - 2
            put_wide(V3U, row + 2, value)
            if -1 <= row < 5:
                VJ[row + 2, :, :ch] = value.astype(BF)

    def second_pair(h):
        both = conv_pair(V3A, h + 3, KB2, h)
        for j in (0, 1):
            act, slope = silu_and_slope(both[:, j * ch : (j + 1) * ch] + b_second)
            if 0 <= h + j < 4:
                S2[h + j] = slope
            put_wide(V3B, h + j + 2, act)
            if -1 <= h + j < 5:
                VJ[h + j + 2, :, ch:] = act.astype(BF)

    def pool(i):
        SB[...] = VJ[2 * i + 2, :, ch:].astype(F32) + VJ[2 * i + 3, :, ch:].astype(F32)
        ref.POOL[i] = (
            (SB[pl.ds(0, half, stride=2), :] + SB[pl.ds(1, half, stride=2), :]) * 0.25
        ).astype(BF)

    def third_pair(h):
        both = conv_pair(V3U, h + 2, KU3, h) + conv_pair(V3B, h + 2, KB3, h)
        for j in (0, 1):
            act, slope = silu_and_slope(both[:, j * ch : (j + 1) * ch] + b_third)
            S3[h + j + 1] = slope
            put_wide(V3C, h + j + 1, act)
            VC[h + j + 2] = act.astype(BF)

    def turn(bank, back, part, lo=0):
        for row_tap in range(3):
            taps_of = bank[1 + row_tap].reshape(3, part, ch)
            for col_tap in range(3):
                back[3 - row_tap, lo : lo + part, (2 - col_tap) * ch : (3 - col_tap) * ch] = taps_of[col_tap]

    wait(in_x)
    wait(in_w1)
    wait(in_co)
    wait(in_up)
    for row in (4, 5, 6, 7):
        widen_input(row)
    first_pair(1)
    up_rows(1)
    up_rows(2)
    start_near(co_halo)
    wait(in_w2)
    wait(in_w3)
    wait(in_w4)
    turn(KB4, KT4, ch)
    turn(KU3, KT3, ch)
    turn(KB3, KT3, ch, ch)
    turn(KB2, KT2, ch)
    turn(KB1, KT1, c_in)
    wait(in_cot)
    wait(in_cp)

    receive_far(x_halo)
    receive_far(co_halo)
    for row in (8, 9, 10, 11):
        widen_input(row)
    first_pair(3)
    first_pair(5)
    up_rows(3)
    second_pair(2)
    second_pair(4)
    third_pair(3)

    receive_near(x_halo)
    receive_near(co_halo)
    for row in (0, 1, 2, 3):
        widen_input(row)
    first_pair(-1)
    first_pair(-3)
    up_rows(0)
    second_pair(0)
    second_pair(-2)
    third_pair(1)
    third_pair(-1)

    G34, G33, G32, G31 = ref.G34, ref.G33, ref.G32, ref.G31
    COT, ACT = ref.COT, ref.ACT
    sums = {}

    def add_sum(layer, value):
        part = jnp.sum(value.reshape(-1, 8, ch), axis=0)
        sums[layer] = part if layer not in sums else sums[layer] + part

    def fourth_pair(h, send):
        both = conv_pair(V3C, h + 1, KB4, h)
        pending = []
        for j in (0, 1):
            act, slope = silu_and_slope(both[:, j * ch : (j + 1) * ch] + b_fourth)
            g = (COT[h + j].astype(F32) * slope).astype(BF)
            G4[h + j + 2] = g
            ACT[h + j] = act.astype(BF)
            pending.append(g)
        send(g4_halo)
        for j in (0, 1):
            g = pending[j].astype(F32)
            add_sum(FOURTH, g)
            put_wide(G34, h + j + 2, g)

    fourth_pair(0, start_near)
    fourth_pair(2, start_far)
    out_act = [fetch(ACT.at[row], ref.activations.at[0, flip(row, 3)]) for row in range(4)]

    class Reduction:
        def __init__(self, index, name):
            self.part, self.twin = getattr(ref, "P_" + name), getattr(ref, "RA_" + name)
            self.sums, self.along = getattr(ref, "Q_" + name), getattr(ref, "RB_" + name)
            self.total, self.slots = getattr(ref, "T_" + name), getattr(ref, "RC_" + name)
            self.index, self.name = index, name

        def copy(self, phase, step, src, dst, device):
            place = self.index, 4 * phase + step
            return remote(src, dst, ref.red_send.at[place], ref.red_recv.at[place], device)

        def to_core(self):
            if fused:
                self.core = self.copy(0, 0, self.part.at[1 - k], self.twin, far_id)
                self.core.start()

        def join_core(self):
            self.core.wait_recv()
            return self.part[k].astype(F32) + self.twin[...].astype(F32)

        def scatter(self, phase, own, n, src, dst, device):
            found = []
            for step in range(1, n):
                other = lax.rem(own + step, n)
                found.append(self.copy(phase, step, src.at[other], dst.at[own], device(other)))
                found[-1].start()
            return found

        def gather(self, phase, src):
            found = []
            for step in range(1, canvas_n):
                other = lax.rem(c + step, canvas_n)
                found.append(self.copy(phase, step, src, self.slots.at[c], (other, r)))
                found[-1].start()
            self.own = fetch(src, self.slots.at[c])
            return found

        def collect(self, copies, own, n, src, dst):
            for copy in copies:
                copy.wait_recv()
            total = src[own].astype(F32)
            for step in range(1, n):
                total = total + dst[lax.rem(own + step, n)].astype(F32)
            return total

        def second(self):
            if fused:
                self.sums[...] = self.join_core().astype(BF)
                self.z_copies = self.scatter(1, z, z_n, self.sums, self.along, lambda other: (c, other * 2 + k))

        def third(self):
            if fused:
                total = self.collect(self.z_copies, z, z_n, self.sums, self.along)
                self.total[...] = total.astype(BF)
                self.last = self.gather(2, self.total)

        def fourth(self):
            pass

        def finish(self):
            if not fused:
                fetch(self.part, self.slots).wait()
                return
            self.core.wait_send()
            for copy in self.z_copies:
                copy.wait_send()
            for copy in self.last:
                copy.wait()
            self.own.wait()

    class WideReduction(Reduction):
        def second(self):
            if fused:
                total = self.join_core()
                quarter = total.shape[1] // canvas_n
                for place in range(canvas_n):
                    self.sums[place] = total[:, place * quarter : (place + 1) * quarter].astype(BF)
                self.c_copies = self.scatter(1, c, canvas_n, self.sums, self.along, lambda other: (other, r))

        def third(self):
            if fused:
                total = self.collect(self.c_copies, c, canvas_n, self.sums, self.along)
                self.zs, self.zl = getattr(ref, "ZS_" + self.name), getattr(ref, "ZL_" + self.name)
                self.zs[...] = total.astype(BF)
                self.z_copies = self.scatter(2, z, z_n, self.zs, self.zl, lambda other: (c, other * 2 + k))

        def fourth(self):
            if fused:
                total = self.collect(self.z_copies, z, z_n, self.zs, self.zl)
                self.total[...] = total.astype(BF)
                self.last = self.gather(3, self.total)

        def finish(self):
            if fused:
                for copy in self.c_copies:
                    copy.wait_send()
            super().finish()

    red = {
        name: (WideReduction if name in WIDE else Reduction)(index, name) for index, name in enumerate(GROUPS)
    }

    def put_parts(name, value, lanes):
        part = getattr(ref, "P_" + name)
        blocks = value.shape[0] // ch
        for block in range(blocks):
            first = (block if name == UP else blocks - 1 - block) * len(lanes)
            for owner in range(8):
                lo = block * ch + owner * 16
                for place, lane in enumerate(lanes):
                    part[owner % 2, owner // 2, first + place] = value[
                        lo : lo + 16, lane * 128 : (lane + 1) * 128
                    ].astype(BF)

    def above_below(h, off, closed):
        above = closed + link(h) * (h - 1 + off - closed)
        below = closed + link(h + 1) * (h + 1 + off - closed)
        return jnp.where(k == 0, above, below), jnp.where(k == 0, below, above)

    def row_stack(src, h):
        above, below = above_below(h, 2, 0)
        return jnp.concatenate([src[above], src[h + 2], src[below]], axis=1)

    def weight_grad(grad3, at, src, lo=0, n=4):
        rows = grad3[at + lo : at + lo + n].reshape(n * width, 3 * ch)
        stacked = jnp.concatenate([row_stack(src, lo + h) for h in range(n)], axis=0)
        return dot_tn(rows, stacked)

    def load_wide(dst, row, src):
        put_wide(dst, row + 2, src[row + 2].astype(F32))

    def third_back(h):
        both = back_pair(G34, h + 2, KT4, h)
        for j in (0, 1):
            g = (both[:, j * ch : (j + 1) * ch] * S3[h + j + 1]).astype(BF).astype(F32)
            if 0 <= h + j < 4:
                add_sum(THIRD, g)
            put_wide(G33, h + j + 1, g)

    put_parts(FOURTH, weight_grad(G34, 2, VC), (0, 1, 2))
    red[FOURTH].to_core()
    third_back(1)
    pool(0)
    pool(1)
    out_pool = [fetch(ref.POOL.at[i], ref.pooled.at[0, flip(i, 1)]) for i in (0, 1)]
    receive_far(g4_halo)
    load_wide(G34, 4, G4)
    load_wide(G34, 5, G4)
    third_back(3)
    ref.far_third[...] = weight_grad(G33, 1, VJ, 1, 3)
    red[FOURTH].second()
    receive_near(g4_halo)
    load_wide(G34, -1, G4)
    load_wide(G34, -2, G4)
    third_back(-1)

    GB, CP = ref.GB, ref.CP

    def joined_back(i, sends):
        spread = CP[i].astype(F32) * 0.25
        SB[pl.ds(0, half, stride=2), :] = spread
        SB[pl.ds(1, half, stride=2), :] = spread
        pending = []
        for a, send in enumerate(sends):
            row = 2 * i + a
            d_joined = back_row(G33, row + 1, KT3, row)
            g = ((d_joined[:, ch:] + SB[...]) * S2[row]).astype(BF)
            G2[row + 2] = g
            send()
            pending.append((a, row, d_joined[:, :ch], g))
        for a, row, d_up, g in pending:
            g_up = d_up.astype(BF).astype(F32)
            add_sum(UP, g_up)
            SA[a] = g_up
            for b in (0, 1):
                GB[i, a, :, b * ch : (b + 1) * ch] = SA[a, pl.ds(b, half, stride=2), :].astype(BF)
            g = g.astype(F32)
            add_sum(SECOND, g)
            put_wide(G32, row + 2, g)

    joined_back(0, (lambda: start_near(g2_halo), lambda: start_near(g2_second)))
    grad = ref.far_third[...] + weight_grad(G33, 1, VJ, 0, 1)
    put_parts(THIRD_B, grad, (1, 3, 5))
    red[THIRD_B].to_core()
    put_parts(THIRD_A, grad, (0, 2, 4))
    red[THIRD_A].to_core()
    joined_back(1, (lambda: start_far(g2_second), lambda: start_far(g2_halo)))

    def bands(i, first, second):
        return jnp.concatenate([GB[i, first], GB[i, second]], axis=1)

    red[THIRD_B].second()
    red[THIRD_A].second()
    put_parts(SECOND, weight_grad(G32, 2, VA), (0, 1, 2))
    red[SECOND].to_core()
    grad = dot_tn(
        jnp.concatenate([bands(0, k, 1 - k), bands(1, k, 1 - k)], axis=0), CO[1:3].reshape(2 * half, c_coarse)
    )
    put_parts(UP, grad, (0, 1))
    red[UP].to_core()

    def first_back(h):
        both = back_pair(G32, h + 2, KT2, h)
        for j in (0, 1):
            g = (both[:, j * ch : (j + 1) * ch] * S1[h + j + 1]).astype(BF).astype(F32)
            add_sum(FIRST, g)
            put_wide(G31, h + j + 1, g)

    def first_back_row(row):
        put_wide(G31, row + 1, (back_row(G32, row + 2, KT2, row) * S1[row + 1]).astype(BF).astype(F32))

    def first_grad(lo):
        stacks = []
        for h in (lo, lo + 1):
            above, below = above_below(h, 4, 12)
            stacks.append(jnp.concatenate([X[above], X[h + 4], X[below]], axis=0))
        rows = G31[lo + 1 : lo + 3].reshape(2 * width, 3 * ch)
        return dot_nn(jnp.concatenate(stacks, axis=1), rows)

    receive_far(g2_halo)
    receive_far(g2_second)
    load_wide(G32, 4, G2)
    load_wide(G32, 5, G2)
    first_back(2)
    ref.far_first[...] = first_grad(2)
    red[SECOND].second()
    red[FOURTH].third()
    red[UP].second()
    receive_near(g2_halo)
    load_wide(G32, -1, G2)
    first_back(0)

    grad = (ref.far_first[...] + first_grad(0)).T
    put_parts(FIRST, jnp.concatenate([grad, jnp.zeros((3 * ch, 256 - 3 * c_in), F32)], axis=1), (0, 1))
    DB = ref.DB
    DB[...] = jnp.zeros(DB.shape, F32)
    for place, layer in enumerate(ORDER):
        DB[place : place + 1] = jnp.sum(sums[layer], axis=0, keepdims=True)
    for owner in range(8):
        ref.P_first[owner % 2, owner // 2, 6] = DB[...].astype(BF)
    red[FIRST].to_core()

    GI, GC = ref.GI, ref.GC

    def input_back(h):
        both = dot_nt(back_weights(KT1, h), band(G31, h + 1)).astype(BF)
        GI[h] = both[:c_in]
        GI[h + 1] = both[c_in:]

    receive_near(g2_second)
    load_wide(G32, -2, G2)
    first_back_row(-1)
    first_back_row(4)
    red[FIRST].second()
    red[THIRD_A].third()
    input_back(0)
    input_back(2)
    out_gi = [fetch(GI.at[row], ref.grad_inputs.at[0, flip(row, 3)]) for row in range(4)]
    red[THIRD_B].third()
    red[FOURTH].fourth()
    for i in (0, 1):
        GC[i] = dot_nt(bands(i, 0, 1), WU[...]).astype(BF)
    out_gc = [fetch(GC.at[i], ref.grad_coarse.at[0, flip(i, 1)]) for i in (0, 1)]
    red[SECOND].third()
    red[UP].third()
    red[THIRD_A].fourth()
    red[THIRD_B].fourth()
    red[FIRST].third()
    red[SECOND].fourth()
    red[UP].fourth()

    for name in GROUPS:
        red[name].finish()
    for pairs in (x_halo, co_halo, g4_halo, g2_halo, g2_second):
        sent(pairs)
    for copies in (out_pool, out_act, out_gi, out_gc):
        wait(copies)


def finish_kernel(names, staged, sizes, *refs):
    ref = types.SimpleNamespace(**dict(zip(names, refs)))
    held = types.SimpleNamespace(**dict(zip(staged, refs[len(names) : -1])))
    sem = refs[-1]
    ch, share = sizes
    r = lax.axis_index("rows")
    enter, leave = {}, {}
    for place, name in enumerate(staged):
        stage = getattr(held, name)
        if name in BIG or name.startswith("RC"):
            enter[name] = pltpu.make_async_copy(getattr(ref, name), stage, sem.at[0, place])
            enter[name].start()
        if name in BIG or name.startswith("w"):
            leave[name] = pltpu.make_async_copy(stage, getattr(ref, "out_" + name), sem.at[1, place])

    def tiles(name):
        slots = getattr(held, "RC_" + name)
        if name in WIDE:
            quarter = slots.shape[1]
            return lambda t: slots[t // quarter, t % quarter].astype(F32)

        def total(t):
            value = slots[0, t].astype(F32)
            for place in range(1, slots.shape[0]):
                value = value + slots[place, t].astype(F32)
            return value

        return total

    for name in BIG:
        enter[name].wait()
        leave[name].start()
    for name in GROUPS:
        enter["RC_" + name].wait()
        tile = tiles(name)
        if name == FIRST:
            out = held.w_first
            part = out.shape[3]
            for col_tap in range(3):
                for row_tap in range(3):
                    value = tile(2 * col_tap + row_tap // 2)
                    lo = part * (row_tap % 2)
                    out[row_tap, col_tap] = value[:, lo : lo + part]
            sums = pltpu.roll(tile(6), lax.rem(ch - r * share, ch), 1)
            for place, layer in enumerate(ORDER):
                getattr(ref, "out_b_" + layer)[...] = sums[place : place + 1, :share]
        layer = name.split("_")[0]
        out = getattr(held, "w_" + layer)
        if name == UP:
            for place in range(4):
                for lane in (0, 1):
                    out[place // 2, place % 2, :, lane * 128 : (lane + 1) * 128] = tile(2 * place + lane)
        elif name != FIRST:
            lo = 128 * (name == THIRD_B)
            for col_tap in range(3):
                for row_tap in range(3):
                    out[row_tap, col_tap, :, lo : lo + 128] = tile(3 * col_tap + row_tap)
        if name != THIRD_A:
            leave["w_" + layer].start()
    for copy in leave.values():
        copy.wait()


def on_device(
    fused,
    rows_n,
    canvas_n,
    inputs,
    coarse,
    row_cuts,
    col_cuts,
    w_first,
    b_first,
    w_second,
    b_second,
    w_up,
    b_up,
    w_third,
    b_third,
    w_fourth,
    b_fourth,
    cot_out,
    cot_pool,
):
    arg = dict(
        inputs=inputs,
        coarse=coarse,
        row_cuts=row_cuts,
        col_cuts=col_cuts,
        w_first=w_first,
        b_first=b_first,
        w_second=w_second,
        b_second=b_second,
        w_up=w_up,
        b_up=b_up,
        w_third=w_third,
        b_third=b_third,
        w_fourth=w_fourth,
        b_fourth=b_fourth,
        cot_out=cot_out,
        cot_pool=cot_pool,
    )
    _, length, width, c_in = arg["inputs"].shape
    ch = arg["w_first"].shape[3]
    c_coarse = arg["coarse"].shape[3]
    half = width // 2
    assert length == 4
    arg["inputs"] = jnp.swapaxes(arg["inputs"], 2, 3)
    arg["w_first"] = arg["w_first"].reshape(3, 3 * c_in, ch)
    arg["w_second"] = arg["w_second"].reshape(3, 3 * ch, ch)
    arg["w_fourth"] = arg["w_fourth"].reshape(3, 3 * ch, ch)
    for name in ORDER:
        name = "b_" + name
        arg[name] = arg[name].reshape(1, ch)

    any_spec = pl.BlockSpec(memory_space=pl.ANY)
    vmem_spec = pl.BlockSpec(memory_space=pltpu.VMEM)
    in_specs = []
    for name in arg:
        if name == "row_cuts":
            in_specs.append(pl.BlockSpec(memory_space=pltpu.SMEM))
        elif name == "col_cuts" or name.startswith("b_"):
            in_specs.append(vmem_spec)
        else:
            in_specs.append(any_spec)

    owners, z_n = 8, 4
    share = ch // owners
    tiles = dict(fourth=9, third_a=9, third_b=9, second=9, up=8, first=7)
    tiles = {name: -(-count // 4) * 4 if name in WIDE else count for name, count in tiles.items()}
    outs = dict(
        activations=jax.ShapeDtypeStruct((1, 4, width, ch), BF),
        pooled=jax.ShapeDtypeStruct((1, 2, half, ch), BF),
        grad_inputs=jax.ShapeDtypeStruct((1, 4, c_in, width), BF),
        grad_coarse=jax.ShapeDtypeStruct((1, 2, half, c_coarse), BF),
    )
    scratch = dict(
        X=pltpu.VMEM((13, c_in, width), BF),
        CO=pltpu.VMEM((4, half, c_coarse), BF),
        COT=pltpu.VMEM((4, width, ch), BF),
        CP=pltpu.VMEM((2, half, ch), BF),
        WU=pltpu.VMEM((c_coarse, 4 * ch), BF),
        GL=pltpu.VMEM((width, ch), F32),
        GR=pltpu.VMEM((width, ch), F32),
        KB1=pltpu.VMEM((4, 3 * c_in, ch), BF),
        KB2=pltpu.VMEM((4, 3 * ch, ch), BF),
        KU3=pltpu.VMEM((4, 3, ch, ch), BF),
        KB3=pltpu.VMEM((4, 3, ch, ch), BF),
        KB4=pltpu.VMEM((4, 3 * ch, ch), BF),
        KT1=pltpu.VMEM((4, c_in, 3 * ch), BF),
        KT2=pltpu.VMEM((4, ch, 3 * ch), BF),
        KT3=pltpu.VMEM((4, 2 * ch, 3 * ch), BF),
        KT4=pltpu.VMEM((4, ch, 3 * ch), BF),
        V3X=pltpu.VMEM((12, 3 * c_in, width), BF),
        V3A=pltpu.VMEM((10, width, 3 * ch), BF),
        V3U=pltpu.VMEM((8, width, 3 * ch), BF),
        V3B=pltpu.VMEM((8, width, 3 * ch), BF),
        V3C=pltpu.VMEM((6, width, 3 * ch), BF),
        VA=pltpu.VMEM((7, width, ch), BF),
        VJ=pltpu.VMEM((7, width, 2 * ch), BF),
        VC=pltpu.VMEM((7, width, ch), BF),
        S1=pltpu.VMEM((6, width, ch), F32),
        S2=pltpu.VMEM((4, width, ch), F32),
        S3=pltpu.VMEM((6, width, ch), F32),
        G4=pltpu.VMEM((8, width, ch), BF),
        G2=pltpu.VMEM((8, width, ch), BF),
        G34=pltpu.VMEM((8, width, 3 * ch), BF),
        G33=pltpu.VMEM((6, width, 3 * ch), BF),
        G32=pltpu.VMEM((8, width, 3 * ch), BF),
        G31=pltpu.VMEM((6, width, 3 * ch), BF),
        far_third=pltpu.VMEM((3 * ch, 6 * ch), F32),
        far_first=pltpu.VMEM((3 * c_in, 3 * ch), F32),
        GB=pltpu.VMEM((2, 2, half, 2 * ch), BF),
        SA=pltpu.VMEM((2, width, ch), F32),
        SB=pltpu.VMEM((width, ch), F32),
        DB=pltpu.VMEM((16, ch), F32),
        ACT=pltpu.VMEM((4, width, ch), BF),
        POOL=pltpu.VMEM((2, half, ch), BF),
        GI=pltpu.VMEM((4, c_in, width), BF),
        GC=pltpu.VMEM((2, half, c_coarse), BF),
        local_sem=pltpu.SemaphoreType.DMA((64,)),
        halo_send=pltpu.SemaphoreType.DMA((9, 2)),
        halo_recv=pltpu.SemaphoreType.DMA((9, 2)),
        red_send=pltpu.SemaphoreType.DMA((6, 16)),
        red_recv=pltpu.SemaphoreType.DMA((6, 16)),
    )
    for name, count in tiles.items():

        def buffer(*lead):
            return pltpu.VMEM(lead + (16, 128), BF)

        landing = (canvas_n, count, 16, 128)
        scratch["P_" + name] = buffer(2, z_n, count)
        scratch["RA_" + name] = buffer(z_n, count)
        if name in WIDE:
            quarter = count // 4
            scratch["Q_" + name] = buffer(4, z_n, quarter)
            scratch["RB_" + name] = buffer(4, z_n, quarter)
            scratch["ZS_" + name] = buffer(z_n, quarter)
            scratch["ZL_" + name] = buffer(z_n, quarter)
            scratch["T_" + name] = buffer(quarter)
            landing = (4, quarter, 16, 128)
        else:
            scratch["Q_" + name] = buffer(z_n, count)
            scratch["RB_" + name] = buffer(z_n, count)
            scratch["T_" + name] = buffer(count)
        if not fused:
            landing = (2, z_n, count, 16, 128)
        outs["RC_" + name] = jax.ShapeDtypeStruct(landing, BF)

    names = list(arg) + list(outs) + list(scratch)
    sizes = (width, ch, c_in, c_coarse, rows_n, canvas_n, fused)
    results = pl.pallas_call(
        functools.partial(level_kernel, names, sizes),
        out_shape=tuple(outs.values()),
        in_specs=in_specs,
        out_specs=tuple(any_spec for _ in outs),
        scratch_shapes=list(scratch.values()),
        compiler_params=pltpu.CompilerParams(
            collective_id=0, has_side_effects=True, vmem_limit_bytes=VMEM_BYTES
        ),
        name="level",
    )(*(arg[name] for name in arg))
    held = dict(zip(outs, results))

    if not fused:
        return unfused_tail(held, rows_n, ch, c_in, c_coarse)

    done = {"out_" + name: outs[name] for name in BIG}
    parts = dict(first=c_in, second=ch, third=2 * ch, fourth=ch)
    for name in ORDER:
        shape = (2, 2, share, c_coarse) if name == UP else (3, 3, share, parts[name])
        done["out_w_" + name] = jax.ShapeDtypeStruct(shape, F32)
    for name in ORDER:
        done["out_b_" + name] = jax.ShapeDtypeStruct((1, share), F32)
    staged = {name: outs[name] for name in outs}
    staged.update({"w_" + name: done["out_w_" + name] for name in ORDER})
    finals = pl.pallas_call(
        functools.partial(finish_kernel, list(outs) + list(done), list(staged), (ch, share)),
        out_shape=tuple(done.values()),
        in_specs=[any_spec] * len(outs),
        out_specs=tuple(vmem_spec if name.startswith("out_b") else any_spec for name in done),
        scratch_shapes=[pltpu.VMEM(like.shape, like.dtype) for like in staged.values()]
        + [pltpu.SemaphoreType.DMA((2, len(staged)))],
        name="finish",
    )(*results)
    final = dict(zip(done, finals))
    return ordered(
        {name: final["out_" + name] for name in BIG},
        {name: final["out_w_" + name] for name in ORDER},
        {name: final["out_b_" + name].reshape(share) for name in ORDER},
    )


def ordered(big, weights, biases):
    turned = {name: jnp.swapaxes(value, 2, 3) for name, value in weights.items()}
    pairs = []
    for name in ORDER:
        pairs += [turned[name], biases[name]]
    return (
        big["activations"],
        big["pooled"],
        jnp.swapaxes(big["grad_inputs"], 2, 3),
        big["grad_coarse"],
        *pairs,
    )


def unfused_tail(held, rows_n, ch, c_in, c_coarse):
    share = ch // rows_n
    offset = lax.axis_index("rows") * share

    def whole(name):
        parts = held["RC_" + name].astype(F32)
        return jnp.transpose(parts, (2, 1, 0, 3, 4)).reshape(-1, ch, 128)

    tiles = lax.psum({name: whole(name) for name in GROUPS}, ("canvas", "rows"))
    weights = {}
    for name in ORDER:
        if name == UP:
            value = tiles[UP].reshape(4, 1, 2, ch, 128)
        elif name == FIRST:
            value = jnp.swapaxes(tiles[name][:6].reshape(3, 2, ch, 128), 1, 2).reshape(3, ch, 256)
            value = jnp.transpose(value[..., : 3 * c_in].reshape(3, ch, 3, c_in), (0, 2, 1, 3))[:, :, None]
        else:
            sides = (THIRD_A, THIRD_B) if name == THIRD else (name,)
            value = jnp.stack([tiles[side][:9].reshape(3, 3, ch, 128) for side in sides], axis=2)
        value = jnp.transpose(value, (1, 0, 3, 2, 4)).reshape(value.shape[1], value.shape[0], ch, -1)
        if name == UP:
            value = value.reshape(2, 2, ch, c_coarse)
        weights[name] = lax.dynamic_slice_in_dim(value, offset, share, 2)
    biases = lax.dynamic_slice_in_dim(tiles[FIRST][6], offset, share, 1)
    return ordered(held, weights, {name: biases[place] for place, name in enumerate(ORDER)})


def solution(mesh):
    rows_n, canvas_n = mesh.shape["rows"], mesh.shape["canvas"]
    fused = rows_n == 8 and canvas_n == 4
    split = P("canvas", "rows", None, None)
    pairs = (P(None, None, None, "rows"), P("rows"))
    return jax.shard_map(
        functools.partial(on_device, fused, rows_n, canvas_n),
        mesh=mesh,
        in_specs=(split, split, P("canvas", None), P("canvas", None)) + (P(),) * 10 + (split, split),
        out_specs=(split,) * 4 + pairs * 5,
        check_vma=False,
    )
```

time: 52.1 us -> 48.4 us (0.929)
  Pallas kernels: 51.1 us -> 47.4 us
    pallas_call x1, Pallas kernels: 48.3 us -> 44.6 us  [on_device(): pl.pallas_call(functools.partial(level_kernel, names, sizes), out_shape=t...]
where the time goes in v3:
time: 48.4 us; the launch traced here: 48.2 us
  Pallas kernels  47.4 us (98%)
  between operations  0.82 us (2%)
    pallas_call x1, Pallas kernels, on_device(): pl.pallas_call(functools.partial(level_kernel, names, sizes), out_shape=t...  44.6 us
    pallas_call x1, Pallas kernels, on_device(): pl.pallas_call(functools.partial(finish_kernel, list(outs) + list(done),...  2.85 us

profile of v3, /device:TPU:0, one launch (start us, length us, event | category | flops | bytes accessed | tf_op | source)
XLA Modules:
  0.0 48.2 jit_solution(18267891229886308834)
XLA Ops:
  0.7 44.6 %level.1 = (bf16[1,4,384,128]{3,2,1,0:T(8,128)(2,1)}, bf16[1,2,192,128]{3,2,1,0:T(8,128)(2,1)}, bf16[1,4,64,384]{3,2,1,0:T(8,128)(2,1)}, bf16[1,2,192,256]{3,2,1...) custom-call(bf16[1,4,64,384]{3,2,1,0:T(8,128)(2,1)} %bitcast.22, ...), custom_call_target="tpu_custom_call" | custom-call | tf_op jit(solution)/shard_map/level/pallas_call | solution.py:878
  45.2 2.9 %finish.1 = (bf16[1,4,384,128]{3,2,1,0:T(8,128)(2,1)}, bf16[1,2,192,128]{3,2,1,0:T(8,128)(2,1)}, bf16[1,4,64,384]{3,2,1,0:T(8,128)(2,1)}, bf16[1,2,192,256]{3,2,...) custom-call(bf16[1,4,384,128]{3,2,1,0:T(8,128)(2,1)} %get-tuple-elem, ...), custom_call_target="tpu_custom_call" | custom-call | tf_op jit(solution)/shard_map/finish/pallas_call | solution.py:903

commit v4 on v3

--- a/solution.py
+++ b/solution.py
@@ -19,6 +19,14 @@
 WIDE = (FOURTH, THIRD_A, SECOND, UP)
 ORDER = (FIRST, SECOND, UP, THIRD, FOURTH)
 BIG = ("activations", "pooled", "grad_inputs", "grad_coarse")
+
+
+def place_of(layer, tile):
+    if layer == THIRD:
+        return (THIRD_A, tile) if tile < 8 else (THIRD_B, tile - 8)
+    if layer == SECOND and tile == 8:
+        return FIRST, 6
+    return layer, tile
 
 
 def dot_nn(a, b):
@@ -190,10 +198,7 @@
     for bank in (KB1, KB2, KU3, KB3, KB4, KT1, KT2, KT3, KT4, ref.VA, ref.VJ, ref.VC):
         bank[0] = jnp.zeros(bank.shape[1:], BF)
     X[12] = jnp.zeros(X.shape[1:], BF)
-    for part in (ref.P_fourth, ref.P_third_a, ref.P_third_b, ref.P_second):
-        if part.shape[2] > 9:
-            part[:, :, 9:] = jnp.zeros(part.shape[:2] + (part.shape[2] - 9,) + part.shape[3:], BF)
-
+    ref.P_fourth[:, :, 9:] = jnp.zeros((2, ref.P_fourth.shape[1], 3, 16, 128), BF)
     peers = (z_n - 1 + canvas_n - 1) if fused else 0
     pl.semaphore_wait(barrier, peers + 1 + has_near.astype(jnp.int32))
     start_near(x_halo)
@@ -443,16 +448,22 @@
         def fourth(self):
             pass
 
+        def settle_first(self):
+            if fused:
+                self.core.wait_send()
+
+        def settle_z(self):
+            if fused:
+                for copy in self.z_copies:
+                    copy.wait_send()
+
         def finish(self):
             if not fused:
                 fetch(self.part, self.slots).wait()
                 return
-            self.core.wait_send()
-            for copy in self.z_copies:
-                copy.wait_send()
+            self.own.wait()
             for copy in self.last:
                 copy.wait()
-            self.own.wait()
 
     class WideReduction(Reduction):
         def second(self):
@@ -476,27 +487,30 @@
                 self.total[...] = total.astype(BF)
                 self.last = self.gather(3, self.total)
 
-        def finish(self):
+        def settle_first(self):
             if fused:
+                self.core.wait_send()
                 for copy in self.c_copies:
                     copy.wait_send()
-            super().finish()
 
     red = {
         name: (WideReduction if name in WIDE else Reduction)(index, name) for index, name in enumerate(GROUPS)
     }
 
-    def put_parts(name, value, lanes):
-        part = getattr(ref, "P_" + name)
-        blocks = value.shape[0] // ch
+    def put_tile(group, index, value):
+        part = getattr(ref, "P_" + group)
+        for owner in range(8):
+            part[owner % 2, owner // 2, index] = value[16 * owner : 16 * owner + 16].astype(BF)
+
+    def put_grad(layer, value):
+        blocks, lanes = value.shape[0] // ch, value.shape[1] // 128
         for block in range(blocks):
-            first = (block if name == UP else blocks - 1 - block) * len(lanes)
-            for owner in range(8):
-                lo = block * ch + owner * 16
-                for place, lane in enumerate(lanes):
-                    part[owner % 2, owner // 2, first + place] = value[
-                        lo : lo + 16, lane * 128 : (lane + 1) * 128
-                    ].astype(BF)
+            first = (block if layer == UP else blocks - 1 - block) * lanes
+            for lane in range(lanes):
+                put_tile(
+                    *place_of(layer, first + lane),
+                    value[block * ch : (block + 1) * ch, lane * 128 : (lane + 1) * 128],
+                )
 
     def above_below(h, off, closed):
         above = closed + link(h) * (h - 1 + off - closed)
@@ -523,7 +537,7 @@
                 add_sum(THIRD, g)
             put_wide(G33, h + j + 1, g)
 
-    put_parts(FOURTH, weight_grad(G34, 2, VC), (0, 1, 2))
+    put_grad(FOURTH, weight_grad(G34, 2, VC))
     red[FOURTH].to_core()
     third_back(1)
     pool(0)
@@ -565,10 +579,8 @@
             put_wide(G32, row + 2, g)
 
     joined_back(0, (lambda: start_near(g2_halo), lambda: start_near(g2_second)))
-    grad = ref.far_third[...] + weight_grad(G33, 1, VJ, 0, 1)
-    put_parts(THIRD_B, grad, (1, 3, 5))
+    put_grad(THIRD, ref.far_third[...] + weight_grad(G33, 1, VJ, 0, 1))
     red[THIRD_B].to_core()
-    put_parts(THIRD_A, grad, (0, 2, 4))
     red[THIRD_A].to_core()
     joined_back(1, (lambda: start_far(g2_second), lambda: start_far(g2_halo)))
 
@@ -577,12 +589,12 @@
 
     red[THIRD_B].second()
     red[THIRD_A].second()
-    put_parts(SECOND, weight_grad(G32, 2, VA), (0, 1, 2))
+    put_grad(SECOND, weight_grad(G32, 2, VA))
     red[SECOND].to_core()
     grad = dot_tn(
         jnp.concatenate([bands(0, k, 1 - k), bands(1, k, 1 - k)], axis=0), CO[1:3].reshape(2 * half, c_coarse)
     )
-    put_parts(UP, grad, (0, 1))
+    put_grad(UP, grad)
     red[UP].to_core()
 
     def first_back(h):
@@ -608,8 +620,8 @@
     load_wide(G32, 4, G2)
     load_wide(G32, 5, G2)
     first_back(2)
+    red[SECOND].second()
     ref.far_first[...] = first_grad(2)
-    red[SECOND].second()
     red[FOURTH].third()
     red[UP].second()
     receive_near(g2_halo)
@@ -617,13 +629,17 @@
     first_back(0)
 
     grad = (ref.far_first[...] + first_grad(0)).T
-    put_parts(FIRST, jnp.concatenate([grad, jnp.zeros((3 * ch, 256 - 3 * c_in), F32)], axis=1), (0, 1))
+    rest = [grad[lo : lo + ch, 128:] for lo in (2 * ch, ch, 0)]
+    for tap in range(3):
+        put_tile(FIRST, tap, grad[(2 - tap) * ch : (3 - tap) * ch, :128])
+    put_tile(FIRST, 3, jnp.concatenate(rest[:2], axis=1))
+    put_tile(FIRST, 4, jnp.concatenate([rest[2], jnp.zeros(rest[2].shape, F32)], axis=1))
     DB = ref.DB
     DB[...] = jnp.zeros(DB.shape, F32)
     for place, layer in enumerate(ORDER):
         DB[place : place + 1] = jnp.sum(sums[layer], axis=0, keepdims=True)
     for owner in range(8):
-        ref.P_first[owner % 2, owner // 2, 6] = DB[...].astype(BF)
+        ref.P_first[owner % 2, owner // 2, 5] = DB[...].astype(BF)
     red[FIRST].to_core()
 
     GI, GC = ref.GI, ref.GC
@@ -633,34 +649,42 @@
         GI[h] = both[:c_in]
         GI[h + 1] = both[c_in:]
 
+    red[THIRD_A].third()
     receive_near(g2_second)
     load_wide(G32, -2, G2)
     first_back_row(-1)
+    red[FIRST].second()
     first_back_row(4)
-    red[FIRST].second()
-    red[THIRD_A].third()
     input_back(0)
     input_back(2)
     out_gi = [fetch(GI.at[row], ref.grad_inputs.at[0, flip(row, 3)]) for row in range(4)]
     red[THIRD_B].third()
     red[FOURTH].fourth()
+    red[SECOND].third()
+    red[UP].third()
     for i in (0, 1):
         GC[i] = dot_nt(bands(i, 0, 1), WU[...]).astype(BF)
     out_gc = [fetch(GC.at[i], ref.grad_coarse.at[0, flip(i, 1)]) for i in (0, 1)]
-    red[SECOND].third()
-    red[UP].third()
+    for pairs in (x_halo, co_halo, g4_halo, g2_halo, g2_second):
+        sent(pairs)
+    wait(out_act)
+    wait(out_pool)
+    for name in GROUPS:
+        red[name].settle_first()
     red[THIRD_A].fourth()
-    red[THIRD_B].fourth()
+    red[FOURTH].settle_z()
+    red[THIRD_B].settle_z()
+    red[FOURTH].finish()
+    red[THIRD_B].finish()
     red[FIRST].third()
     red[SECOND].fourth()
     red[UP].fourth()
-
-    for name in GROUPS:
+    wait(out_gi)
+    wait(out_gc)
+    for name in (THIRD_A, FIRST, SECOND, UP):
+        red[name].settle_z()
+    for name in (THIRD_A, FIRST, SECOND, UP):
         red[name].finish()
-    for pairs in (x_halo, co_halo, g4_halo, g2_halo, g2_second):
-        sent(pairs)
-    for copies in (out_pool, out_act, out_gi, out_gc):
-        wait(copies)
 
 
 def finish_kernel(names, staged, sizes, *refs):
@@ -678,50 +702,43 @@
         if name in BIG or name.startswith("w"):
             leave[name] = pltpu.make_async_copy(stage, getattr(ref, "out_" + name), sem.at[1, place])
 
-    def tiles(name):
-        slots = getattr(held, "RC_" + name)
-        if name in WIDE:
+    def tile(group, index):
+        slots = getattr(held, "RC_" + group)
+        if group in WIDE:
             quarter = slots.shape[1]
-            return lambda t: slots[t // quarter, t % quarter].astype(F32)
-
-        def total(t):
-            value = slots[0, t].astype(F32)
-            for place in range(1, slots.shape[0]):
-                value = value + slots[place, t].astype(F32)
-            return value
-
-        return total
+            return slots[index // quarter, index % quarter].astype(F32)
+        value = slots[0, index].astype(F32)
+        for place in range(1, slots.shape[0]):
+            value = value + slots[place, index].astype(F32)
+        return value
 
     for name in BIG:
         enter[name].wait()
         leave[name].start()
     for name in GROUPS:
         enter["RC_" + name].wait()
-        tile = tiles(name)
-        if name == FIRST:
-            out = held.w_first
+    for layer in ORDER:
+        out = getattr(held, "w_" + layer)
+        lanes = out.shape[3] // 128
+        if layer == FIRST:
             part = out.shape[3]
             for col_tap in range(3):
-                for row_tap in range(3):
-                    value = tile(2 * col_tap + row_tap // 2)
-                    lo = part * (row_tap % 2)
-                    out[row_tap, col_tap] = value[:, lo : lo + part]
-            sums = pltpu.roll(tile(6), lax.rem(ch - r * share, ch), 1)
-            for place, layer in enumerate(ORDER):
-                getattr(ref, "out_b_" + layer)[...] = sums[place : place + 1, :share]
-        layer = name.split("_")[0]
-        out = getattr(held, "w_" + layer)
-        if name == UP:
-            for place in range(4):
-                for lane in (0, 1):
-                    out[place // 2, place % 2, :, lane * 128 : (lane + 1) * 128] = tile(2 * place + lane)
-        elif name != FIRST:
-            lo = 128 * (name == THIRD_B)
-            for col_tap in range(3):
-                for row_tap in range(3):
-                    out[row_tap, col_tap, :, lo : lo + 128] = tile(3 * col_tap + row_tap)
-        if name != THIRD_A:
-            leave["w_" + layer].start()
+                whole, rest = tile(FIRST, col_tap), tile(FIRST, 3 + col_tap // 2)
+                lo = part * (col_tap % 2)
+                out[0, col_tap] = whole[:, :part]
+                out[1, col_tap] = whole[:, part:]
+                out[2, col_tap] = rest[:, lo : lo + part]
+        else:
+            for place in range(out.shape[0] * out.shape[1]):
+                col_tap, row_tap = place // out.shape[0], place % out.shape[0]
+                first, second = (col_tap, row_tap) if layer == UP else (row_tap, col_tap)
+                for lane in range(lanes):
+                    value = tile(*place_of(layer, place * lanes + lane))
+                    out[first, second, :, lane * 128 : (lane + 1) * 128] = value
+        leave["w_" + layer].start()
+    sums = pltpu.roll(tile(FIRST, 5), lax.rem(ch - r * share, ch), 1)
+    for place, layer in enumerate(ORDER):
+        getattr(ref, "out_b_" + layer)[...] = sums[place : place + 1, :share]
     for copy in leave.values():
         copy.wait()
 
@@ -791,8 +808,7 @@
 
     owners, z_n = 8, 4
     share = ch // owners
-    tiles = dict(fourth=9, third_a=9, third_b=9, second=9, up=8, first=7)
-    tiles = {name: -(-count // 4) * 4 if name in WIDE else count for name, count in tiles.items()}
+    tiles = dict(fourth=12, third_a=8, third_b=10, second=8, up=8, first=7)
     outs = dict(
         activations=jax.ShapeDtypeStruct((1, 4, width, ch), BF),
         pooled=jax.ShapeDtypeStruct((1, 2, half, ch), BF),
@@ -942,19 +958,20 @@
     tiles = lax.psum({name: whole(name) for name in GROUPS}, ("canvas", "rows"))
     weights = {}
     for name in ORDER:
-        if name == UP:
-            value = tiles[UP].reshape(4, 1, 2, ch, 128)
-        elif name == FIRST:
-            value = jnp.swapaxes(tiles[name][:6].reshape(3, 2, ch, 128), 1, 2).reshape(3, ch, 256)
-            value = jnp.transpose(value[..., : 3 * c_in].reshape(3, ch, 3, c_in), (0, 2, 1, 3))[:, :, None]
+        if name == FIRST:
+            whole_taps = tiles[FIRST][:3]
+            rest = jnp.stack([tiles[FIRST][3][:, :c_in], tiles[FIRST][3][:, c_in:], tiles[FIRST][4][:, :c_in]])
+            value = jnp.stack([whole_taps[..., :c_in], whole_taps[..., c_in:], rest], axis=1)[:, :, None]
         else:
-            sides = (THIRD_A, THIRD_B) if name == THIRD else (name,)
-            value = jnp.stack([tiles[side][:9].reshape(3, 3, ch, 128) for side in sides], axis=2)
+            lanes, shape = (2, (4, 1)) if name == UP else (2 if name == THIRD else 1, (3, 3))
+            count = lanes * shape[0] * shape[1]
+            found = [place_of(name, place) for place in range(count)]
+            value = jnp.stack([tiles[group][index] for group, index in found]).reshape(*shape, lanes, ch, 128)
         value = jnp.transpose(value, (1, 0, 3, 2, 4)).reshape(value.shape[1], value.shape[0], ch, -1)
         if name == UP:
             value = value.reshape(2, 2, ch, c_coarse)
         weights[name] = lax.dynamic_slice_in_dim(value, offset, share, 2)
-    biases = lax.dynamic_slice_in_dim(tiles[FIRST][6], offset, share, 1)
+    biases = lax.dynamic_slice_in_dim(tiles[FIRST][5], offset, share, 1)
     return ordered(held, weights, {name: biases[place] for place, name in enumerate(ORDER)})
 
 

time: 48.4 us -> 47.1 us (0.973)
  Pallas kernels: 47.4 us -> 46.1 us
    pallas_call x1, Pallas kernels: 44.6 us -> 43.1 us  [on_device(): pl.pallas_call(functools.partial(level_kernel, names, sizes), out_shape=t...]
where the time goes in v4:
time: 47.1 us; the launch traced here: 46.9 us
  Pallas kernels  46.1 us (98%)
  between operations  0.82 us (2%)
    pallas_call x1, Pallas kernels, on_device(): pl.pallas_call(functools.partial(level_kernel, names, sizes), out_shape=t...  43.1 us
    pallas_call x1, Pallas kernels, on_device(): pl.pallas_call(functools.partial(finish_kernel, list(outs) + list(done),...  2.96 us

profile of v4, /device:TPU:0, one launch (start us, length us, event | category | flops | bytes accessed | tf_op | source)
XLA Modules:
  0.0 46.9 jit_solution(4845275725624871687)
XLA Ops:
  0.7 43.1 %level.1 = (bf16[1,4,384,128]{3,2,1,0:T(8,128)(2,1)}, bf16[1,2,192,128]{3,2,1,0:T(8,128)(2,1)}, bf16[1,4,64,384]{3,2,1,0:T(8,128)(2,1)}, bf16[1,2,192,256]{3,2,1...) custom-call(bf16[1,4,64,384]{3,2,1,0:T(8,128)(2,1)} %bitcast.22, ...), custom_call_target="tpu_custom_call" | custom-call | tf_op jit(solution)/shard_map/level/pallas_call | solution.py:894
  43.8 3.0 %finish.1 = (bf16[1,4,384,128]{3,2,1,0:T(8,128)(2,1)}, bf16[1,2,192,128]{3,2,1,0:T(8,128)(2,1)}, bf16[1,4,64,384]{3,2,1,0:T(8,128)(2,1)}, bf16[1,2,192,256]{3,2,...) custom-call(bf16[1,4,384,128]{3,2,1,0:T(8,128)(2,1)} %get-tuple-elem, ...), custom_call_target="tpu_custom_call" | custom-call | tf_op jit(solution)/shard_map/finish/pallas_call | solution.py:919

commit v5 on v4

--- a/solution.py
+++ b/solution.py
@@ -25,7 +25,7 @@
     if layer == THIRD:
         return (THIRD_A, tile) if tile < 8 else (THIRD_B, tile - 8)
     if layer == SECOND and tile == 8:
-        return FIRST, 6
+        return FIRST, 5
     return layer, tile
 
 
@@ -615,6 +615,7 @@
         rows = G31[lo + 1 : lo + 3].reshape(2 * width, 3 * ch)
         return dot_nn(jnp.concatenate(stacks, axis=1), rows)
 
+    red[FOURTH].third()
     receive_far(g2_halo)
     receive_far(g2_second)
     load_wide(G32, 4, G2)
@@ -622,7 +623,6 @@
     first_back(2)
     red[SECOND].second()
     ref.far_first[...] = first_grad(2)
-    red[FOURTH].third()
     red[UP].second()
     receive_near(g2_halo)
     load_wide(G32, -1, G2)
@@ -633,13 +633,14 @@
     for tap in range(3):
         put_tile(FIRST, tap, grad[(2 - tap) * ch : (3 - tap) * ch, :128])
     put_tile(FIRST, 3, jnp.concatenate(rest[:2], axis=1))
-    put_tile(FIRST, 4, jnp.concatenate([rest[2], jnp.zeros(rest[2].shape, F32)], axis=1))
     DB = ref.DB
     DB[...] = jnp.zeros(DB.shape, F32)
     for place, layer in enumerate(ORDER):
-        DB[place : place + 1] = jnp.sum(sums[layer], axis=0, keepdims=True)
-    for owner in range(8):
-        ref.P_first[owner % 2, owner // 2, 5] = DB[...].astype(BF)
+        total = jnp.sum(sums[layer], axis=0, keepdims=True)
+        DB[place : place + 1] = total[:, : ch // 2]
+        DB[5 + place : 6 + place] = total[:, ch // 2 :]
+    spare = jnp.concatenate([DB[...]] * 8, axis=0)
+    put_tile(FIRST, 4, jnp.concatenate([rest[2], spare], axis=1))
     red[FIRST].to_core()
 
     GI, GC = ref.GI, ref.GC
@@ -699,7 +700,7 @@
         if name in BIG or name.startswith("RC"):
             enter[name] = pltpu.make_async_copy(getattr(ref, name), stage, sem.at[0, place])
             enter[name].start()
-        if name in BIG or name.startswith("w"):
+        if not name.startswith("RC"):
             leave[name] = pltpu.make_async_copy(stage, getattr(ref, "out_" + name), sem.at[1, place])
 
     def tile(group, index):
@@ -736,9 +737,12 @@
                     value = tile(*place_of(layer, place * lanes + lane))
                     out[first, second, :, lane * 128 : (lane + 1) * 128] = value
         leave["w_" + layer].start()
-    sums = pltpu.roll(tile(FIRST, 5), lax.rem(ch - r * share, ch), 1)
+    spare = tile(FIRST, 4)[:, ch // 2 :]
+    sums = jnp.concatenate([spare[0:8], spare[5:13]], axis=1)
+    sums = pltpu.roll(sums, lax.rem(ch - r * share, ch), 1)
     for place, layer in enumerate(ORDER):
-        getattr(ref, "out_b_" + layer)[...] = sums[place : place + 1, :share]
+        getattr(held, "b_" + layer)[...] = sums[place : place + 1, :share]
+        leave["b_" + layer].start()
     for copy in leave.values():
         copy.wait()
 
@@ -808,7 +812,7 @@
 
     owners, z_n = 8, 4
     share = ch // owners
-    tiles = dict(fourth=12, third_a=8, third_b=10, second=8, up=8, first=7)
+    tiles = dict(fourth=12, third_a=8, third_b=10, second=8, up=8, first=6)
     outs = dict(
         activations=jax.ShapeDtypeStruct((1, 4, width, ch), BF),
         pooled=jax.ShapeDtypeStruct((1, 2, half, ch), BF),
@@ -854,7 +858,7 @@
         GB=pltpu.VMEM((2, 2, half, 2 * ch), BF),
         SA=pltpu.VMEM((2, width, ch), F32),
         SB=pltpu.VMEM((width, ch), F32),
-        DB=pltpu.VMEM((16, ch), F32),
+        DB=pltpu.VMEM((16, ch // 2), F32),
         ACT=pltpu.VMEM((4, width, ch), BF),
         POOL=pltpu.VMEM((2, half, ch), BF),
         GI=pltpu.VMEM((4, c_in, width), BF),
@@ -916,11 +920,12 @@
         done["out_b_" + name] = jax.ShapeDtypeStruct((1, share), F32)
     staged = {name: outs[name] for name in outs}
     staged.update({"w_" + name: done["out_w_" + name] for name in ORDER})
+    staged.update({"b_" + name: done["out_b_" + name] for name in ORDER})
     finals = pl.pallas_call(
         functools.partial(finish_kernel, list(outs) + list(done), list(staged), (ch, share)),
         out_shape=tuple(done.values()),
         in_specs=[any_spec] * len(outs),
-        out_specs=tuple(vmem_spec if name.startswith("out_b") else any_spec for name in done),
+        out_specs=(any_spec,) * len(done),
         scratch_shapes=[pltpu.VMEM(like.shape, like.dtype) for like in staged.values()]
         + [pltpu.SemaphoreType.DMA((2, len(staged)))],
         name="finish",
@@ -971,7 +976,8 @@
         if name == UP:
             value = value.reshape(2, 2, ch, c_coarse)
         weights[name] = lax.dynamic_slice_in_dim(value, offset, share, 2)
-    biases = lax.dynamic_slice_in_dim(tiles[FIRST][5], offset, share, 1)
+    spare = tiles[FIRST][4][:, ch // 2 :]
+    biases = lax.dynamic_slice_in_dim(jnp.concatenate([spare[0:5], spare[5:10]], axis=1), offset, share, 1)
     return ordered(held, weights, {name: biases[place] for place, name in enumerate(ORDER)})
 
 

time: 47.1 us -> 46.5 us (0.987)
  Pallas kernels: 46.1 us -> 45.5 us
where the time goes in v5:
time: 46.5 us; the launch traced here: 46.3 us
  Pallas kernels  45.5 us (98%)
  between operations  0.82 us (2%)
    pallas_call x1, Pallas kernels, on_device(): pl.pallas_call(functools.partial(level_kernel, names, sizes), out_shape=t...  43 us
    pallas_call x1, Pallas kernels, on_device(): pl.pallas_call(functools.partial(finish_kernel, list(outs) + list(done),...  2.52 us

profile of v5, /device:TPU:0, one launch (start us, length us, event | category | flops | bytes accessed | tf_op | source)
XLA Modules:
  0.0 46.3 jit_solution(520150839259600297)
XLA Ops:
  0.7 43.0 %level.1 = (bf16[1,4,384,128]{3,2,1,0:T(8,128)(2,1)}, bf16[1,2,192,128]{3,2,1,0:T(8,128)(2,1)}, bf16[1,4,64,384]{3,2,1,0:T(8,128)(2,1)}, bf16[1,2,192,256]{3,2,1...) custom-call(bf16[1,4,64,384]{3,2,1,0:T(8,128)(2,1)} %bitcast.22, ...), custom_call_target="tpu_custom_call" | custom-call | tf_op jit(solution)/shard_map/level/pallas_call | solution.py:898
  43.6 2.5 %finish.1 = (bf16[1,4,384,128]{3,2,1,0:T(8,128)(2,1)}, bf16[1,2,192,128]{3,2,1,0:T(8,128)(2,1)}, bf16[1,4,64,384]{3,2,1,0:T(8,128)(2,1)}, bf16[1,2,192,256]{3,2,...) custom-call(bf16[1,4,384,128]{3,2,1,0:T(8,128)(2,1)} %get-tuple-elem, ...), custom_call_target="tpu_custom_call" | custom-call | tf_op jit(solution)/shard_map/finish/pallas_call | solution.py:924

commit v6 on v5

--- a/solution.py
+++ b/solution.py
@@ -27,6 +27,14 @@
     if layer == SECOND and tile == 8:
         return FIRST, 5
     return layer, tile
+
+
+def peer_of(own, step):
+    if step == 3:
+        return 3 - own
+    if step == 2:
+        return lax.rem(own + 2, 4)
+    return own + 1 - 2 * lax.rem(own, 2)
 
 
 def dot_nn(a, b):
@@ -411,16 +419,16 @@
 
         def scatter(self, phase, own, n, src, dst, device):
             found = []
-            for step in range(1, n):
-                other = lax.rem(own + step, n)
+            for step in (3, 2, 1):
+                other = peer_of(own, step)
                 found.append(self.copy(phase, step, src.at[other], dst.at[own], device(other)))
                 found[-1].start()
             return found
 
         def gather(self, phase, src):
             found = []
-            for step in range(1, canvas_n):
-                other = lax.rem(c + step, canvas_n)
+            for step in (3, 2, 1):
+                other = peer_of(c, step)
                 found.append(self.copy(phase, step, src, self.slots.at[c], (other, r)))
                 found[-1].start()
             self.own = fetch(src, self.slots.at[c])

time: 46.5 us -> 47.3 us (1.017)
  Pallas kernels: 45.5 us -> 46.3 us
    pallas_call x1, Pallas kernels: 43 us -> 43.7 us  [on_device(): pl.pallas_call(functools.partial(level_kernel, names, sizes), out_shape=t...]
where the time goes in v6:
time: 47.3 us; the launch traced here: 47.1 us
  Pallas kernels  46.3 us (98%)
  between operations  0.82 us (2%)
    pallas_call x1, Pallas kernels, on_device(): pl.pallas_call(functools.partial(level_kernel, names, sizes), out_shape=t...  43.7 us
    pallas_call x1, Pallas kernels, on_device(): pl.pallas_call(functools.partial(finish_kernel, list(outs) + list(done),...  2.52 us

profile of v6, /device:TPU:0, one launch (start us, length us, event | category | flops | bytes accessed | tf_op | source)
XLA Modules:
  0.0 47.1 jit_solution(2562175905901094517)
XLA Ops:
  0.7 43.7 %level.1 = (bf16[1,4,384,128]{3,2,1,0:T(8,128)(2,1)}, bf16[1,2,192,128]{3,2,1,0:T(8,128)(2,1)}, bf16[1,4,64,384]{3,2,1,0:T(8,128)(2,1)}, bf16[1,2,192,256]{3,2,1...) custom-call(bf16[1,4,64,384]{3,2,1,0:T(8,128)(2,1)} %bitcast.22, ...), custom_call_target="tpu_custom_call" | custom-call | tf_op jit(solution)/shard_map/level/pallas_call | solution.py:906
  44.4 2.5 %finish.1 = (bf16[1,4,384,128]{3,2,1,0:T(8,128)(2,1)}, bf16[1,2,192,128]{3,2,1,0:T(8,128)(2,1)}, bf16[1,4,64,384]{3,2,1,0:T(8,128)(2,1)}, bf16[1,2,192,256]{3,2,...) custom-call(bf16[1,4,384,128]{3,2,1,0:T(8,128)(2,1)} %get-tuple-elem, ...), custom_call_target="tpu_custom_call" | custom-call | tf_op jit(solution)/shard_map/finish/pallas_call | solution.py:932
